TPU v7x, 32 devices: a whole 2x2x4 slice. The times are simulated.
32 devices in a mesh: rad: 4 (over y, x), azi: 8 (over z, core).
Axes of the slice: x: 2, y: 2, z: 4, core: 2. Of those that a mesh axis runs over, the one named last changes fastest.
Arguments:
- tokens: bfloat16 [32, 128, 8, 512], P('rad', 'azi'), may hold values from -6 to 6
- cotangent: bfloat16 [32, 128, 8, 512], P('rad', 'azi'), may hold values from -6 to 6
- ln_gain: float32 [512], replicated, may hold values from 0.5 to 1.5
- qkv_weight: bfloat16 [512, 1536], P('azi'), may hold values from -2 to 2
- out_weight: bfloat16 [512, 512], P('azi'), may hold values from -0.25 to 0.25
- shear_offset: int32 [1], replicated, may hold values from 0 to 127
- window_shift: int32 [3], replicated, may hold values from 1 to 7, as said below
Outputs:
- block_out: bfloat16 [32, 128, 8, 512], P('rad', 'azi')
- grad_tokens: bfloat16 [32, 128, 8, 512], P('rad', 'azi')
- grad_qkv: float32 [512, 1536], P('azi')
- grad_out: float32 [512, 512], P('azi')
- grad_gain: float32 [512], replicated
Inputs may be any that keep to these rules, and one draw needn't show every extreme that they name: `window_shift`: the radial entry lies in 1 to 3; the azimuthal and vertical entries lie in 1 to 7, and one of these two equals 7.
All inputs are finite; a program needn't handle non-finite values.
Results may differ from a plain program's by a relative error of at most 0.025.
Values may be sent and summed in bfloat16 or wider, within the bound.
No kernel may reach another device: no remote copies, remote signals or barrier semaphores. Data moves between devices by JAX's collectives and lax.ppermute only.
A program may use at most 192 MiB of HBM per device.

v0:
```python
import jax
import jax.numpy as jnp
from jax import lax
from jax.sharding import PartitionSpec as P

HEADS = 16
HD = 32
WR = 4
WA = 8
WZ = 8


EPS = 1e-05


def shifted_2(block, axis, distance):
    devices = range(lax.axis_size(axis))
    route = [((i - distance) % len(devices), i) for i in devices]
    return lax.ppermute(block, axis, route)


def to_windows(tensor, parts):
    extent_r, extent_a, extent_z, channels = tensor.shape
    tensor = tensor.reshape(
        extent_r // WR, WR, extent_a // WA, WA, extent_z // WZ, WZ, parts, HEADS, HD
    )
    tensor = tensor.transpose(0, 2, 4, 6, 7, 1, 3, 5, 8)
    return tensor.reshape(-1, parts, HEADS, WR * WA * WZ, HD)


def from_windows(windows, extent_r, extent_a, extent_z):
    parts = windows.shape[1]
    windows = windows.reshape(
        extent_r // WR, extent_a // WA, extent_z // WZ, parts, HEADS, WR, WA, WZ, HD
    )
    windows = windows.transpose(0, 5, 1, 6, 2, 7, 3, 4, 8)
    return windows.reshape(extent_r, extent_a, extent_z, parts * HEADS * HD)


def azi_roll(pieces, amount):
    cols_dev = pieces[0].shape[1]
    device_hops = amount // cols_dev
    remainder = amount % cols_dev
    current = pieces
    bit_count = (lax.axis_size("azi") - 1).bit_length()
    for bit_level in range(bit_count):
        hopped = shifted_2((current[0], current[1]), "azi", -(1 << bit_level))
        chosen = device_hops >> bit_level & 1 == 1
        current = (
            jnp.where(chosen, hopped[0], current[0]),
            jnp.where(chosen, hopped[1], current[1]),
        )
    following = shifted_2((current[0], current[1]), "azi", -1)
    return tuple(
        (
            lax.dynamic_slice_in_dim(
                jnp.concatenate([mine, theirs], axis=1), remainder, cols_dev, 1
            )
            for mine, theirs in zip(current, following)
        )
    )


def vertical_roll(field, start):
    depth = field.shape[2]
    return lax.dynamic_slice_in_dim(jnp.concatenate([field, field], axis=2), start, depth, 2)


def shift_in(first, second, shift_rad, shift_azi, shift_ver, offset, total_cols):
    rim_rows = WR - 1
    rows_dev, cols_dev, depth, width = first.shape
    below = shifted_2((first[:rim_rows], second[:rim_rows]), "rad", -1)
    extended = (
        jnp.concatenate([first, below[0]], axis=0),
        jnp.concatenate([second, below[1]], axis=0),
    )
    leading = shifted_2((extended[0][:, : WA - 1], extended[1][:, : WA - 1]), "azi", -1)
    rolled = tuple(
        (
            lax.dynamic_slice_in_dim(
                jnp.concatenate([own_part, lead_part], axis=1), shift_azi, cols_dev, 1
            )
            for own_part, lead_part in zip(extended, leading)
        )
    )
    wrapped = azi_roll(below, (offset + shift_azi) % total_cols)
    last_row = lax.axis_index("rad") == lax.axis_size("rad") - 1
    results = []
    for rolled_part, wrapped_part in zip(rolled, wrapped):
        joined = jnp.concatenate(
            [rolled_part[:rows_dev], jnp.where(last_row, wrapped_part, rolled_part[rows_dev:])],
            axis=0,
        )
        joined = lax.dynamic_slice_in_dim(joined, shift_rad, rows_dev, 0)
        results.append(vertical_roll(joined, shift_ver))
    return (results[0], results[1])


def shift_out(first, second, shift_rad, shift_azi, shift_ver, offset, total_cols):
    rim_rows = WR - 1
    rows_dev, cols_dev, depth, width = first.shape
    above = shifted_2((first[rows_dev - rim_rows :], second[rows_dev - rim_rows :]), "rad", 1)
    extended = (
        jnp.concatenate([above[0], first], axis=0),
        jnp.concatenate([above[1], second], axis=0),
    )
    trailing = shifted_2(
        (extended[0][:, cols_dev - (WA - 1) :], extended[1][:, cols_dev - (WA - 1) :]), "azi", 1
    )
    rolled = tuple(
        (
            lax.dynamic_slice_in_dim(
                jnp.concatenate([trail_part, own_part], axis=1), WA - 1 - shift_azi, cols_dev, 1
            )
            for own_part, trail_part in zip(extended, trailing)
        )
    )
    amount = (total_cols - (offset + shift_azi) % total_cols) % total_cols
    wrapped = azi_roll(above, amount)
    first_row = lax.axis_index("rad") == 0
    results = []
    for rolled_part, wrapped_part in zip(rolled, wrapped):
        joined = jnp.concatenate(
            [jnp.where(first_row, wrapped_part, rolled_part[:rim_rows]), rolled_part[rim_rows:]],
            axis=0,
        )
        joined = lax.dynamic_slice_in_dim(joined, rim_rows - shift_rad, rows_dev, 0)
        results.append(vertical_roll(joined, depth - shift_ver))
    return (results[0], results[1])


def on_device(tokens, cotangent, ln_gain, qkv_weight, out_weight, shear_offset, window_shift):
    rows_dev, cols_dev, depth, width = tokens.shape
    number = rows_dev * cols_dev * depth
    n_rad = lax.axis_size("rad")
    n_azi = lax.axis_size("azi")
    total_cols = cols_dev * n_azi
    shift_rad = window_shift[0]
    shift_azi = window_shift[1]
    shift_ver = window_shift[2]
    offset = shear_offset[0]
    contract = (((0,), (0,)), ((), ()))
    scaling = HD ** (-0.5)
    shifted, grad_in = shift_in(
        tokens, cotangent, shift_rad, shift_azi, shift_ver, offset, total_cols
    )
    inputs_f = shifted.astype(jnp.float32).reshape(number, width)
    centre = jnp.mean(inputs_f, axis=1, keepdims=True)
    centred = inputs_f - centre
    variance = jnp.mean(centred * centred, axis=1, keepdims=True)
    inverse_std = lax.rsqrt(variance + EPS)
    normed = centred * inverse_std
    hidden = (normed * ln_gain).astype(jnp.bfloat16)
    qkv_full, out_full = (
        lax.all_gather(qkv_weight, "azi", axis=0, tiled=True),
        lax.all_gather(out_weight, "azi", axis=0, tiled=True),
    )
    qkv = jnp.dot(hidden, qkv_full, preferred_element_type=jnp.float32)
    qkv = qkv.astype(jnp.bfloat16)
    windows = to_windows(qkv.reshape(rows_dev, cols_dev, depth, 3 * width), 3)
    queries, keys_win, values = (windows[:, 0], windows[:, 1], windows[:, 2])
    scores = (
        jnp.einsum("nhqd,nhkd->nhqk", queries, keys_win, preferred_element_type=jnp.float32)
        * scaling
    )
    weights = jax.nn.softmax(scores, axis=-1)
    weights_low = weights.astype(jnp.bfloat16)
    mixed = jnp.einsum(
        "nhqk,nhkd->nhqd", weights_low, values, preferred_element_type=jnp.float32
    ).astype(jnp.bfloat16)
    attended = from_windows(mixed[:, None], rows_dev, cols_dev, depth).reshape(number, width)
    branch = jnp.dot(attended, out_full, preferred_element_type=jnp.float32)
    out_shifted = (inputs_f + branch).astype(jnp.bfloat16)
    grad_low = grad_in.reshape(number, width)
    d_attended = jnp.dot(grad_low, out_full.T, preferred_element_type=jnp.float32)
    d_attended = d_attended.astype(jnp.bfloat16)
    d_windows = to_windows(d_attended.reshape(rows_dev, cols_dev, depth, width), 1)[:, 0]
    d_weights = jnp.einsum("nhqd,nhkd->nhqk", d_windows, values, preferred_element_type=jnp.float32)
    d_values = jnp.einsum(
        "nhqk,nhqd->nhkd", weights_low, d_windows, preferred_element_type=jnp.float32
    )
    d_scores = (
        weights * (d_weights - jnp.sum(weights * d_weights, axis=-1, keepdims=True))
    ).astype(jnp.bfloat16)
    d_queries = (
        jnp.einsum("nhqk,nhkd->nhqd", d_scores, keys_win, preferred_element_type=jnp.float32)
        * scaling
    )
    d_keys = (
        jnp.einsum("nhqk,nhqd->nhkd", d_scores, queries, preferred_element_type=jnp.float32)
        * scaling
    )
    d_stack = jnp.stack([d_queries, d_keys, d_values], axis=1).astype(jnp.bfloat16)
    d_qkv = from_windows(d_stack, rows_dev, cols_dev, depth).reshape(number, 3 * width)
    d_hidden = jnp.dot(d_qkv, qkv_full.T, preferred_element_type=jnp.float32)
    d_normed = d_hidden * ln_gain
    d_branch = inverse_std * (
        d_normed
        - jnp.mean(d_normed, axis=1, keepdims=True)
        - normed * jnp.mean(d_normed * normed, axis=1, keepdims=True)
    )
    grad_shifted = (grad_low.astype(jnp.float32) + d_branch).astype(jnp.bfloat16)
    shape_out = (rows_dev, cols_dev, depth, width)
    block_out, grad_tokens = shift_out(
        out_shifted.reshape(shape_out),
        grad_shifted.reshape(shape_out),
        shift_rad,
        shift_azi,
        shift_ver,
        offset,
        total_cols,
    )
    term_qkv = lax.dot_general(hidden, d_qkv, contract, preferred_element_type=jnp.float32)
    term_out = lax.dot_general(attended, grad_low, contract, preferred_element_type=jnp.float32)
    whole_term = lax.psum(jnp.concatenate([term_qkv, term_out], axis=1).astype(jnp.bfloat16), "rad")
    share = lax.psum_scatter(whole_term, "azi", scatter_dimension=0, tiled=True).astype(jnp.float32)
    gain_total = lax.psum(jnp.sum(d_hidden * normed, axis=0), ("rad", "azi"))
    factor = float(number * n_rad * n_azi) ** (-0.5)
    grad_qkv = share[:, : 3 * width] * factor
    grad_out = share[:, 3 * width :] * factor
    return (block_out, grad_tokens, grad_qkv, grad_out, gain_total * factor)


def solution(mesh):
    in_specs = (
        P("rad", "azi", None, None),
        P("rad", "azi", None, None),
        P(),
        P("azi", None),
        P("azi", None),
        P(),
        P(),
    )
    out_specs = (
        P("rad", "azi", None, None),
        P("rad", "azi", None, None),
        P("azi", None),
        P("azi", None),
        P(),
    )
    return jax.shard_map(
        on_device, mesh=mesh, in_specs=in_specs, out_specs=out_specs, check_vma=False
    )
```

profile of v0, /device:TPU:0, one launch (start us, length us, event | category | flops | bytes accessed | tf_op | source)
XLA Modules:
  0.0 544.7 jit_solution(6369260182149009998)
XLA Ops:
  8.4 3.9 collective-permute-start.12
  14.7 7.2 %collective-permute-done.12 = bf16[3,16,8,512]{3,2,1,0:T(8,128)(2,1)} collective-permute-done((bf16[3,16,8,512]{3,2,1,0:T(8,128)(2,1)S(1)}, bf16[3,16,8,512]{3,2,1,0:T(8,128)(2,1)}, u32[]{:S(2)}, u32[]{:S(2)}) %collective-permute-start.12) | collective-permute-done | bytes 393248 | tf_op jit(solution)/shard_map/ppermute | solution.py:19
  30.8 2.7 collective-permute-start.2
  33.7 3.4 collective-permute-done.14
  38.2 2.3 collective-permute-start.15
  44.5 5.6 %collective-permute-start.3 = (bf16[3,16,8,512]{3,2,1,0:T(8,128)(2,1)S(1)}, bf16[3,16,8,512]{3,2,1,0:T(8,128)(2,1)S(1)}, u32[]{:S(2)}, u32[]{:S(2)}) collective-permute-start(bf16[3,16,8,512]{3,2,1,0:T(8,128)(2,1)S(1)} %get-tuple-element.12), channel_id=1, source_target_pairs={{2,0},{3,1},{4,2},{5,3},{6,4},{7,5},{0,6},{1,7},{10,8},{11,9},{12,... | collective-permute-start | bytes 1179656 | tf_op jit(solution)/shard_map/ppermute | solution.py:19
  50.2 31.0 %all_gather.7 = bf16[512,512]{1,0:T(8,128)(2,1)S(1)} all-gather(bf16[64,512]{1,0:T(8,128)(2,1)S(1)} %copy-done.16), channel_id=1, replica_groups=mesh['rad'=4,'azi'=8] {'azi'}, dimensions={0}, use_global_device_ids=true | all-gather | bytes 589824 | tf_op jit(solution)/shard_map/all_gather | solution.py:156
  82.2 2.7 collective-permute-start.4
  85.4 34.4 %collective-permute-done.16 = bf16[3,16,8,512]{3,2,1,0:T(8,128)(2,1)S(1)} collective-permute-done((bf16[3,16,8,512]{3,2,1,0:T(8,128)(2,1)S(1)}, bf16[3,16,8,512]{3,2,1,0:T(8,128)(2,1)S(1)}, u32[]{:S(2)}, u32[]{:S(2)}) %collective-permute-start.16) | collective-permute-done | bytes 393248 | tf_op jit(solution)/shard_map/ppermute | solution.py:19
  120.5 3.6 collective-permute-done.4
  129.2 6.4 %reshape_reshape.14 = bf16[2,4,2,8,1,8,1,16,32]{8,7,5,3,2,1,0,6,4:T(8,128)(2,1)} reshape(bf16[1024,512]{1,0:T(8,128)(2,1)} %convolution_convert_fusion.2) | data formatting | bytes 2097152 | tf_op jit(solution)/shard_map/reshape;reshape | solution.py:24
  135.6 5.3 copy.26
  145.9 3.5 convolution_convert_fusion
  149.4 9.9 %reshape_reshape.12 = bf16[2,4,2,8,1,8,3,16,32]{8,7,6,5,3,2,1,0,4:T(8,128)(2,1)} reshape(bf16[1024,1536]{1,0:T(8,128)(2,1)S(1)} %convolution_convert_fusion) | data formatting | bytes 6291456 | tf_op jit(solution)/shard_map/reshape;reshape | solution.py:24
  159.3 12.8 %copy.19 = bf16[2,4,2,8,1,8,3,16,32]{8,5,3,1,7,6,2,0,4:T(8,128)(2,1)} copy(bf16[2,4,2,8,1,8,3,16,32]{8,7,6,5,3,2,1,0,4:T(8,128)(2,1)} %reshape_reshape.12) | data formatting | bytes 6291456 | tf_op jit(solution)/shard_map/reshape;reshape | solution.py:24
  172.1 11.5 %fusion.11 = f32[4,16,256,256]{2,3,1,0:T(8,128)} fusion(bf16[4,3,16,256,32]{4,3,2,1,0:T(8,128)(2,1)} %bitcast.105), kind=kOutput, calls=%fused_computation.19 | convolution fusion | flops 268435456 | bytes 25165824 | tf_op jit(solution)/shard_map/nhqd,nhkd->nhqk/dot_general | solution.py:163
  183.6 19.4 %fusion.62 = (f32[4,16,256]{2,1,0:T(8,128)S(1)}, f32[4,16,256,256]{2,3,1,0:T(8,128)}) fusion(f32[4,16,256,256]{2,3,1,0:T(8,128)} %fusion.11), kind=kOutput, calls=%fused_computation.135 | output fusion | flops 16777472 | bytes 33619968 | tf_op jit(solution)/shard_map/sub | solution.py:166
  203.0 14.4 %multiply_reduce_fusion = (f32[4,16,256]{2,1,0:T(8,128)S(1)}, f32[4,16,256,256]{2,3,1,0:T(8,128)}) fusion(f32[4,16,256,256]{2,3,1,0:T(8,128)} %get-tuple-element.18, f32[4,16,256]{2,1,0:T(8,128)S(1)} %get-tuple-element.17, bf16[4,16,256,32]{3,2,1,0:T(8,128)(2,1)} %bitcast.120, bf16[4,3,16,256,32]{4,3,2,1,0:T(8,128)(2,1)} %bitcast.106), kind=kOutput, calls=%fused_computation.2 | convolution fusion | flops 281001984 | bytes 42074112 | tf_op jit(solution)/shard_map/nhqd,nhkd->nhqk/dot_general | solution.py:178
  217.4 11.7 %multiply_convert_fusion = bf16[4,16,256,256]{2,3,1,0:T(8,128)(2,1)S(1)} fusion(f32[4,16,256,256]{2,3,1,0:T(8,128)} %get-tuple-element.20, f32[4,16,256]{2,1,0:T(8,128)S(1)} %get-tuple-element.19, f32[4,16,256,256]{2,3,1,0:T(8,128)} %get-tuple-element.18, f32[4,16,256]{2,1,0:T(8,128)S(1)} %get-tuple-element.17), kind=kLoop, calls=%fused_computation.1 | loop fusion | flops 16777216 | bytes 42074112 | tf_op jit(solution)/shard_map/convert_element_type | solution.py:184
  229.1 3.3 copy-done
  232.4 3.7 multiply_convert_fusion.2
  236.1 7.3 %multiply_convert_fusion.1 = bf16[4,16,256,32]{2,3,1,0:T(8,128)(2,1)S(1)} fusion(bf16[4,16,256,256]{2,3,1,0:T(8,128)(2,1)} %copy-done, bf16[4,3,16,256,32]{4,3,2,1,0:T(8,128)(2,1)} %bitcast.108), kind=kOutput, calls=%fused_computation.53 | convolution fusion | flops 269484032 | bytes 13631488 | tf_op jit(solution)/shard_map/nhqk,nhqd->nhkd/dot_general | solution.py:190
  243.4 8.5 %fusion.34 = bf16[4,16,256,32]{2,3,1,0:T(8,128)(2,1)} fusion(bf16[4,16,256,32]{3,2,1,0:T(8,128)(2,1)S(1)} %bitcast.121, f32[4,16,256,256]{2,3,1,0:T(8,128)} %get-tuple-element.18, f32[4,16,256]{2,1,0:T(8,128)S(1)} %get-tuple-element.17), kind=kOutput, calls=%fused_computation.67 | convolution fusion | flops 277348352 | bytes 18939904 | tf_op jit(solution)/shard_map/nhqk,nhqd->nhkd/dot_general | solution.py:179
  251.9 9.7 %fusion.31 = bf16[4,16,256,32]{2,3,1,0:T(8,128)(2,1)} fusion(bf16[4,3,16,256,32]{4,3,2,1,0:T(8,128)(2,1)} %bitcast.109, f32[4,16,256,256]{2,3,1,0:T(8,128)} %get-tuple-element.18, f32[4,16,256]{2,1,0:T(8,128)S(1)} %get-tuple-element.17), kind=kOutput, calls=%fused_computation.66 | convolution fusion | flops 277348352 | bytes 22085632 | tf_op jit(solution)/shard_map/nhqk,nhkd->nhqd/dot_general | solution.py:168
  261.5 3.2 copy.29
  264.7 3.1 copy.31
  267.8 3.1 copy.34
  270.9 6.0 %maximum_bitcast_fusion = bf16[2,4,2,8,1,8,3,16,32]{8,5,3,1,7,2,0,6,4:T(8,128)(2,1)S(1)} fusion(bf16[2,2,1,1,16,4,8,8,32]{8,7,6,5,4,1,0,3,2:T(8,128)(2,1)} %bitcast.113, bf16[2,2,1,1,16,4,8,8,32]{8,7,6,5,4,1,0,3,2:T(8,128)(2,1)} %bitcast.112, bf16[2,2,1,1,16,4,8,8,32]{8,7,6,5,4,1,0,3,2:T(8,128)(2,1)} %bitcast.111), kind=kLoop, calls=%fused_computation.6 | loop fusion | flops 3145728 | bytes 6291456 | tf_op jit(solution)/shard_map/transpose | solution.py:36
  277.0 16.6 %copy.35 = bf16[2,4,2,8,1,8,3,16,32]{8,7,6,5,3,2,1,0,4:T(8,128)(2,1)} copy(bf16[2,4,2,8,1,8,3,16,32]{8,5,3,1,7,2,0,6,4:T(8,128)(2,1)S(1)} %maximum_bitcast_fusion) | data formatting | bytes 6291456 | tf_op jit(solution)/shard_map/transpose | solution.py:36
  293.6 17.1 %reshape_reshape.15 = bf16[1024,1536]{1,0:T(8,128)(2,1)} reshape(bf16[2,4,2,8,1,8,3,16,32]{8,7,6,5,3,2,1,0,4:T(8,128)(2,1)} %copy.35) | data formatting | bytes 6291456 | tf_op jit(solution)/shard_map/reshape;reshape | solution.py:194
  310.6 3.1 copy.24
  313.7 10.8 %copy.25 = bf16[2,4,2,8,1,8,1,16,32]{8,7,5,3,2,1,0,6,4:T(8,128)(2,1)} copy(bf16[2,4,2,8,1,8,1,16,32]{8,5,3,1,7,2,0,6,4:T(8,128)(2,1)} %bitcast.110) | data formatting | bytes 2097152 | tf_op jit(solution)/shard_map/transpose | solution.py:36
  324.5 6.2 %reshape_reshape.13 = bf16[1024,512]{1,0:T(8,128)(2,1)S(1)} reshape(bf16[2,4,2,8,1,8,1,16,32]{8,7,5,3,2,1,0,6,4:T(8,128)(2,1)} %copy.25) | data formatting | bytes 2097152 | tf_op jit(solution)/shard_map/reshape;reshape | solution.py:171
  338.0 4.6 fusion.29
  347.8 7.1 %collective-permute-done.18 = bf16[3,16,8,512]{3,2,1,0:T(8,128)(2,1)S(1)} collective-permute-done((bf16[3,16,8,512]{3,2,1,0:T(8,128)(2,1)S(1)}, bf16[3,16,8,512]{3,2,1,0:T(8,128)(2,1)S(1)}, u32[]{:S(2)}, u32[]{:S(2)}) %collective-permute-start.18) | collective-permute-done | bytes 393248 | tf_op jit(solution)/shard_map/ppermute | solution.py:19
  354.9 10.3 %collective-permute-start.19 = (bf16[3,16,8,512]{3,2,1,0:T(8,128)(2,1)S(1)}, bf16[3,16,8,512]{3,2,1,0:T(8,128)(2,1)}, u32[]{:S(2)}, u32[]{:S(2)}) collective-permute-start(bf16[3,16,8,512]{3,2,1,0:T(8,128)(2,1)S(1)} %collective-permute-done.18), channel_id=1, source_target_pairs={{1,0},{2,1},{3,2},{4,3},{5,4},{6,5},{7,6},{0,7},{9,8},{10,9},{11,1... | collective-permute-start | bytes 1179656 | tf_op jit(solution)/shard_map/ppermute | solution.py:19
  368.9 37.3 %psum.15 = f32[512]{0:T(512)S(1)} all-reduce(f32[512]{0:T(512)S(1)} %get-tuple-element.5), channel_id=1, replica_groups=mesh['rad'=4,'azi'=8] {'rad','azi'}, use_global_device_ids=true, to_apply=%region_10.11 | all-reduce | flops 512 | bytes 4096 | tf_op jit(solution)/shard_map/psum | solution.py:217
  407.7 2.1 collective-permute-start.20
  410.1 6.1 %collective-permute-done.7 = bf16[3,16,8,512]{3,2,1,0:T(8,128)(2,1)S(1)} collective-permute-done((bf16[3,16,8,512]{3,2,1,0:T(8,128)(2,1)S(1)}, bf16[3,16,8,512]{3,2,1,0:T(8,128)(2,1)S(1)}, u32[]{:S(2)}, u32[]{:S(2)}) %collective-permute-start.7) | collective-permute-done | bytes 393248 | tf_op jit(solution)/shard_map/ppermute | solution.py:19
  418.3 12.8 %collective-permute-done.20 = bf16[3,16,8,512]{3,2,1,0:T(8,128)(2,1)S(1)} collective-permute-done((bf16[3,16,8,512]{3,2,1,0:T(8,128)(2,1)S(1)}, bf16[3,16,8,512]{3,2,1,0:T(8,128)(2,1)S(1)}, u32[]{:S(2)}, u32[]{:S(2)}) %collective-permute-start.20) | collective-permute-done | bytes 393248 | tf_op jit(solution)/shard_map/ppermute | solution.py:19
  431.8 2.5 collective-permute-done.23
  434.7 10.4 %collective-permute-done.8 = bf16[3,16,8,512]{3,2,1,0:T(8,128)(2,1)S(1)} collective-permute-done((bf16[3,16,8,512]{3,2,1,0:T(8,128)(2,1)S(1)}, bf16[3,16,8,512]{3,2,1,0:T(8,128)(2,1)S(1)}, u32[]{:S(2)}, u32[]{:S(2)}) %collective-permute-start.8) | collective-permute-done | bytes 393248 | tf_op jit(solution)/shard_map/ppermute | solution.py:19
  445.1 15.8 %collective-permute-start.9 = (bf16[3,16,8,512]{3,2,1,0:T(8,128)(2,1)S(1)}, bf16[3,16,8,512]{3,2,1,0:T(8,128)(2,1)S(1)}, u32[]{:S(2)}, u32[]{:S(2)}) collective-permute-start(bf16[3,16,8,512]{3,2,1,0:T(8,128)(2,1)S(1)} %broadcast_select_fusion.9), channel_id=1, source_target_pairs={{4,0},{5,1},{6,2},{7,3},{0,4},{1,5},{2,6},{3,7},{12,8},{13,9},{14,... | collective-permute-start | bytes 1179656 | tf_op jit(solution)/shard_map/ppermute | solution.py:19
  460.9 13.1 %collective-permute-done.21 = bf16[3,16,8,512]{3,2,1,0:T(8,128)(2,1)S(1)} collective-permute-done((bf16[3,16,8,512]{3,2,1,0:T(8,128)(2,1)S(1)}, bf16[3,16,8,512]{3,2,1,0:T(8,128)(2,1)S(1)}, u32[]{:S(2)}, u32[]{:S(2)}) %collective-permute-start.21) | collective-permute-done | bytes 393248 | tf_op jit(solution)/shard_map/ppermute | solution.py:19
  476.0 3.6 collective-permute-done.9
  479.6 5.7 %collective-permute-start.10 = (bf16[3,16,8,512]{3,2,1,0:T(8,128)(2,1)S(1)}, bf16[3,16,8,512]{3,2,1,0:T(8,128)(2,1)S(1)}, u32[]{:S(2)}, u32[]{:S(2)}) collective-permute-start(bf16[3,16,8,512]{3,2,1,0:T(8,128)(2,1)S(1)} %broadcast_select_fusion.11), channel_id=1, source_target_pairs={{1,0},{2,1},{3,2},{4,3},{5,4},{6,5},{7,6},{0,7},{9,8},{10,9},{11,1... | collective-permute-start | bytes 1179656 | tf_op jit(solution)/shard_map/ppermute | solution.py:19
  487.5 3.1 collective-permute-done.10
  492.9 42.4 %all-reduce.2.cloned.1.call-done = bf16[64,2048]{1,0:T(8,128)(2,1)} async-done(((bf16[64,2048]{1,0:T(8,128)(2,1)}), bf16[64,2048]{1,0:T(8,128)(2,1)}) %all-reduce.2.cloned.1.call-update) | async-done | bytes 262160 | tf_op jit(solution)/shard_map/psum | solution.py:215
  (141 shorter events, 49.1 us)
Async XLA Ops:
  7.2 23.5 %copy-start.7 = (bf16[8,16,8,512]{3,2,1,0:T(8,128)(2,1)S(1)}, bf16[8,16,8,512]{3,2,1,0:T(8,128)(2,1)}, u32[]{:S(2)}) copy-start(bf16[8,16,8,512]{3,2,1,0:T(8,128)(2,1)} %param.8) | copy-start | bytes 3145732
  7.2 26.4 %copy-start.8 = (bf16[8,16,8,512]{3,2,1,0:T(8,128)(2,1)S(1)}, bf16[8,16,8,512]{3,2,1,0:T(8,128)(2,1)}, u32[]{:S(2)}) copy-start(bf16[8,16,8,512]{3,2,1,0:T(8,128)(2,1)} %param.7) | copy-start | bytes 3145732
  7.2 138.7 %all-gather.2.cloned.1.call-start = ((), (), s32[]{:S(2)}) async-start(), calls=%async_computation.1 | async-start | bytes 1769472 | tf_op jit(solution)/shard_map/all_gather | solution.py:155
  8.4 13.5 %collective-permute-start.12 = (bf16[3,16,8,512]{3,2,1,0:T(8,128)(2,1)S(1)}, bf16[3,16,8,512]{3,2,1,0:T(8,128)(2,1)}, u32[]{:S(2)}, u32[]{:S(2)}) collective-permute-start(bf16[3,16,8,512]{3,2,1,0:T(8,128)(2,1)S(1)} %slice.93), channel_id=1, source_target_pairs={{8,0},{16,8},{24,16},{0,24},{9,1},{17,9},{25,17},{1,25},{10,2},{18... | collective-permute-start | bytes 1179656 | tf_op jit(solution)/shard_map/ppermute | solution.py:19
  13.4 17.4 %collective-permute-start = (bf16[3,16,8,512]{3,2,1,0:T(8,128)(2,1)S(1)}, bf16[3,16,8,512]{3,2,1,0:T(8,128)(2,1)S(1)}, u32[]{:S(2)}, u32[]{:S(2)}) collective-permute-start(bf16[3,16,8,512]{3,2,1,0:T(8,128)(2,1)S(1)} %slice.79), channel_id=1, source_target_pairs={{8,0},{16,8},{24,16},{0,24},{9,1},{17,9},{25,17},{1,25},{10,2},{18... | collective-permute-start | bytes 1179656 | tf_op jit(solution)/shard_map/ppermute | solution.py:19
  14.0 476.9 %reduce-scatter.2.cloned.1.call-start = ((), (), s32[]{:S(2)}) async-start(), calls=%async_computation.2 | async-start | bytes 2359296 | tf_op jit(solution)/shard_map/reduce_scatter | solution.py:216
  21.9 15.2 %collective-permute-start.14 = (bf16[3,16,8,512]{3,2,1,0:T(8,128)(2,1)}, bf16[3,16,8,512]{3,2,1,0:T(8,128)(2,1)S(1)}, u32[]{:S(2)}, u32[]{:S(2)}) collective-permute-start(bf16[3,16,8,512]{3,2,1,0:T(8,128)(2,1)} %collective-permute-done.12), channel_id=1, source_target_pairs={{1,0},{2,1},{3,2},{4,3},{5,4},{6,5},{7,6},{0,7},{9,8},{10,9},{11,1... | collective-permute-start | bytes 1179656 | tf_op jit(solution)/shard_map/ppermute | solution.py:19
  30.8 13.6 %collective-permute-start.2 = (bf16[3,16,8,512]{3,2,1,0:T(8,128)(2,1)S(1)}, bf16[3,16,8,512]{3,2,1,0:T(8,128)(2,1)S(1)}, u32[]{:S(2)}, u32[]{:S(2)}) collective-permute-start(bf16[3,16,8,512]{3,2,1,0:T(8,128)(2,1)S(1)} %collective-permute-done), channel_id=1, source_target_pairs={{1,0},{2,1},{3,2},{4,3},{5,4},{6,5},{7,6},{0,7},{9,8},{10,9},{11,1... | collective-permute-start | bytes 1179656 | tf_op jit(solution)/shard_map/ppermute | solution.py:19
  33.7 16.5 %copy-start.16 = (bf16[64,512]{1,0:T(8,128)(2,1)S(1)}, bf16[64,512]{1,0:T(8,128)(2,1)}, u32[]{:S(2)}) copy-start(bf16[64,512]{1,0:T(8,128)(2,1)} %param.11) | copy-start | bytes 196612
  38.2 43.6 %collective-permute-start.15 = (bf16[3,16,8,512]{3,2,1,0:T(8,128)(2,1)S(1)}, bf16[3,16,8,512]{3,2,1,0:T(8,128)(2,1)S(1)}, u32[]{:S(2)}, u32[]{:S(2)}) collective-permute-start(bf16[3,16,8,512]{3,2,1,0:T(8,128)(2,1)S(1)} %get-tuple-element.10), channel_id=1, source_target_pairs={{2,0},{3,1},{4,2},{5,3},{6,4},{7,5},{0,6},{1,7},{10,8},{11,9},{12,... | collective-permute-start | bytes 1179656 | tf_op jit(solution)/shard_map/ppermute | solution.py:19
  40.5 44.4 %collective-permute-start.13 = (bf16[11,7,8,512]{3,2,1,0:T(8,128)(2,1)S(1)}, bf16[11,7,8,512]{3,2,1,0:T(8,128)(2,1)S(1)}, u32[]{:S(2)}, u32[]{:S(2)}) collective-permute-start(bf16[11,7,8,512]{3,2,1,0:T(8,128)(2,1)S(1)} %slice.113), channel_id=1, source_target_pairs={{1,0},{2,1},{3,2},{4,3},{5,4},{6,5},{7,6},{0,7},{9,8},{10,9},{11,1... | collective-permute-start | bytes 1892360 | tf_op jit(solution)/shard_map/ppermute | solution.py:19
  44.5 37.6 %collective-permute-start.3 = (bf16[3,16,8,512]{3,2,1,0:T(8,128)(2,1)S(1)}, bf16[3,16,8,512]{3,2,1,0:T(8,128)(2,1)S(1)}, u32[]{:S(2)}, u32[]{:S(2)}) collective-permute-start(bf16[3,16,8,512]{3,2,1,0:T(8,128)(2,1)S(1)} %get-tuple-element.12), channel_id=1, source_target_pairs={{2,0},{3,1},{4,2},{5,3},{6,4},{7,5},{0,6},{1,7},{10,8},{11,9},{12,... | collective-permute-start | bytes 1179656 | tf_op jit(solution)/shard_map/ppermute | solution.py:19
  81.2 45.3 %copy-start.14 = (bf16[512,512]{1,0:T(8,128)(2,1)}, bf16[512,512]{1,0:T(8,128)(2,1)S(1)}, u32[]{:S(2)}) copy-start(bf16[512,512]{1,0:T(8,128)(2,1)S(1)} %all_gather.7) | copy-start | bytes 1572868
  81.3 38.7 %collective-permute-start.1 = (bf16[11,7,8,512]{3,2,1,0:T(8,128)(2,1)S(1)}, bf16[11,7,8,512]{3,2,1,0:T(8,128)(2,1)S(1)}, u32[]{:S(2)}, u32[]{:S(2)}) collective-permute-start(bf16[11,7,8,512]{3,2,1,0:T(8,128)(2,1)S(1)} %slice.104), channel_id=1, source_target_pairs={{1,0},{2,1},{3,2},{4,3},{5,4},{6,5},{7,6},{0,7},{9,8},{10,9},{11,1... | collective-permute-start | bytes 1892360 | tf_op jit(solution)/shard_map/ppermute | solution.py:19
  81.8 38.0 %collective-permute-start.16 = (bf16[3,16,8,512]{3,2,1,0:T(8,128)(2,1)S(1)}, bf16[3,16,8,512]{3,2,1,0:T(8,128)(2,1)S(1)}, u32[]{:S(2)}, u32[]{:S(2)}) collective-permute-start(bf16[3,16,8,512]{3,2,1,0:T(8,128)(2,1)S(1)} %broadcast_select_fusion.2), channel_id=1, source_target_pairs={{4,0},{5,1},{6,2},{7,3},{0,4},{1,5},{2,6},{3,7},{12,8},{13,9},{14,... | collective-permute-start | bytes 1179656 | tf_op jit(solution)/shard_map/ppermute | solution.py:19
  82.2 41.9 %collective-permute-start.4 = (bf16[3,16,8,512]{3,2,1,0:T(8,128)(2,1)S(1)}, bf16[3,16,8,512]{3,2,1,0:T(8,128)(2,1)S(1)}, u32[]{:S(2)}, u32[]{:S(2)}) collective-permute-start(bf16[3,16,8,512]{3,2,1,0:T(8,128)(2,1)S(1)} %broadcast_select_fusion.3), channel_id=1, source_target_pairs={{4,0},{5,1},{6,2},{7,3},{0,4},{1,5},{2,6},{3,7},{12,8},{13,9},{14,... | collective-permute-start | bytes 1179656 | tf_op jit(solution)/shard_map/ppermute | solution.py:19
  119.9 5.4 collective-permute-start.17
  124.1 16.8 %collective-permute-start.5 = (bf16[3,16,8,512]{3,2,1,0:T(8,128)(2,1)S(1)}, bf16[3,16,8,512]{3,2,1,0:T(8,128)(2,1)S(1)}, u32[]{:S(2)}, u32[]{:S(2)}) collective-permute-start(bf16[3,16,8,512]{3,2,1,0:T(8,128)(2,1)S(1)} %broadcast_select_fusion.5), channel_id=1, source_target_pairs={{1,0},{2,1},{3,2},{4,3},{5,4},{6,5},{7,6},{0,7},{9,8},{10,9},{11,1... | collective-permute-start | bytes 1179656 | tf_op jit(solution)/shard_map/ppermute | solution.py:19
  141.4 1.6 copy-start.21
  142.3 3.6 copy-start.1
  142.4 3.5 copy-start.17
  143.0 2.8 copy-start.19
  229.1 3.3 copy-start
  236.1 7.3 %copy-start.5 = (bf16[2,4,2,8,1,8,1,16,32]{8,5,3,1,7,2,0,6,4:T(8,128)(2,1)S(1)}, bf16[2,4,2,8,1,8,1,16,32]{8,5,3,1,7,2,0,6,4:T(8,128)(2,1)}, u32[]{:S(2)}) copy-start(bf16[2,4,2,8,1,8,1,16,32]{8,5,3,1,7,2,0,6,4:T(8,128)(2,1)} %copy.26) | copy-start | bytes 3145732
  264.7 3.1 copy-start.12
  293.6 17.1 %copy-start.11 = (bf16[4,16,256,32]{2,3,1,0:T(8,128)(2,1)S(1)}, bf16[4,16,256,32]{2,3,1,0:T(8,128)(2,1)}, u32[]{:S(2)}) copy-start(bf16[4,16,256,32]{2,3,1,0:T(8,128)(2,1)} %fusion.31) | copy-start | bytes 3145732
  324.5 6.2 %copy-start.4 = (bf16[8,16,8,512]{3,2,1,0:T(8,128)(2,1)S(1)}, bf16[8,16,8,512]{3,2,1,0:T(8,128)(2,1)}, u32[]{:S(2)}) copy-start(bf16[8,16,8,512]{3,2,1,0:T(8,128)(2,1)} %copy-done.3) | copy-start | bytes 3145732
  330.8 2.3 copy-start.6
  330.8 2.5 copy-start.13
  336.8 1.2 copy-start.2
  336.8 1.2 copy-start.18
  336.8 1.2 copy-start.20
  336.8 1.2 copy-start.22
  336.8 198.4 %all-reduce.2.cloned.1.call-start = ((), (), s32[]{:S(2)}) async-start(), calls=%async_computation.3 | async-start | bytes 524288 | tf_op jit(solution)/shard_map/psum | solution.py:215
  342.6 2.9 copy-start.10
  342.6 2.9 copy-start.15
  343.7 11.2 %collective-permute-start.18 = (bf16[3,16,8,512]{3,2,1,0:T(8,128)(2,1)S(1)}, bf16[3,16,8,512]{3,2,1,0:T(8,128)(2,1)S(1)}, u32[]{:S(2)}, u32[]{:S(2)}) collective-permute-start(bf16[3,16,8,512]{3,2,1,0:T(8,128)(2,1)S(1)} %bitcast.124), channel_id=1, source_target_pairs={{24,0},{0,8},{8,16},{16,24},{25,1},{1,9},{9,17},{17,25},{26,2},{2,... | collective-permute-start | bytes 1179656 | tf_op jit(solution)/shard_map/ppermute | solution.py:19
  346.2 60.5 %collective-permute-start.6 = (bf16[3,16,8,512]{3,2,1,0:T(8,128)(2,1)S(1)}, bf16[3,16,8,512]{3,2,1,0:T(8,128)(2,1)S(1)}, u32[]{:S(2)}, u32[]{:S(2)}) collective-permute-start(bf16[3,16,8,512]{3,2,1,0:T(8,128)(2,1)S(1)} %bitcast.123), channel_id=1, source_target_pairs={{24,0},{0,8},{8,16},{16,24},{25,1},{1,9},{9,17},{17,25},{26,2},{2,... | collective-permute-start | bytes 1179656 | tf_op jit(solution)/shard_map/ppermute | solution.py:19
  354.9 52.8 %collective-permute-start.19 = (bf16[3,16,8,512]{3,2,1,0:T(8,128)(2,1)S(1)}, bf16[3,16,8,512]{3,2,1,0:T(8,128)(2,1)}, u32[]{:S(2)}, u32[]{:S(2)}) collective-permute-start(bf16[3,16,8,512]{3,2,1,0:T(8,128)(2,1)S(1)} %collective-permute-done.18), channel_id=1, source_target_pairs={{1,0},{2,1},{3,2},{4,3},{5,4},{6,5},{7,6},{0,7},{9,8},{10,9},{11,1... | collective-permute-start | bytes 1179656 | tf_op jit(solution)/shard_map/ppermute | solution.py:19
  406.7 9.5 %collective-permute-start.7 = (bf16[3,16,8,512]{3,2,1,0:T(8,128)(2,1)S(1)}, bf16[3,16,8,512]{3,2,1,0:T(8,128)(2,1)S(1)}, u32[]{:S(2)}, u32[]{:S(2)}) collective-permute-start(bf16[3,16,8,512]{3,2,1,0:T(8,128)(2,1)S(1)} %collective-permute-done.6), channel_id=1, source_target_pairs={{1,0},{2,1},{3,2},{4,3},{5,4},{6,5},{7,6},{0,7},{9,8},{10,9},{11,1... | collective-permute-start | bytes 1179656 | tf_op jit(solution)/shard_map/ppermute | solution.py:19
  407.7 23.4 %collective-permute-start.20 = (bf16[3,16,8,512]{3,2,1,0:T(8,128)(2,1)S(1)}, bf16[3,16,8,512]{3,2,1,0:T(8,128)(2,1)S(1)}, u32[]{:S(2)}, u32[]{:S(2)}) collective-permute-start(bf16[3,16,8,512]{3,2,1,0:T(8,128)(2,1)S(1)} %broadcast_select_fusion.6), channel_id=1, source_target_pairs={{2,0},{3,1},{4,2},{5,3},{6,4},{7,5},{0,6},{1,7},{10,8},{11,9},{12,... | collective-permute-start | bytes 1179656 | tf_op jit(solution)/shard_map/ppermute | solution.py:19
  409.9 24.3 %collective-permute-start.23 = (bf16[11,7,8,512]{3,2,1,0:T(8,128)(2,1)S(1)}, bf16[11,7,8,512]{3,2,1,0:T(8,128)(2,1)S(1)}, u32[]{:S(2)}, u32[]{:S(2)}) collective-permute-start(bf16[11,7,8,512]{3,2,1,0:T(8,128)(2,1)S(1)} %pad_maximum_fusion.1), channel_id=1, source_target_pairs={{7,0},{0,1},{1,2},{2,3},{3,4},{4,5},{5,6},{6,7},{15,8},{8,9},{9,10... | collective-permute-start | bytes 1892360 | tf_op jit(solution)/shard_map/ppermute | solution.py:19
  410.0 65.4 %collective-permute-start.11 = (bf16[11,7,8,512]{3,2,1,0:T(8,128)(2,1)S(1)}, bf16[11,7,8,512]{3,2,1,0:T(8,128)(2,1)S(1)}, u32[]{:S(2)}, u32[]{:S(2)}) collective-permute-start(bf16[11,7,8,512]{3,2,1,0:T(8,128)(2,1)S(1)} %pad_maximum_fusion.2), channel_id=1, source_target_pairs={{7,0},{0,1},{1,2},{2,3},{3,4},{4,5},{5,6},{6,7},{15,8},{8,9},{9,10... | collective-permute-start | bytes 1892360 | tf_op jit(solution)/shard_map/ppermute | solution.py:19
  416.2 28.8 %collective-permute-start.8 = (bf16[3,16,8,512]{3,2,1,0:T(8,128)(2,1)S(1)}, bf16[3,16,8,512]{3,2,1,0:T(8,128)(2,1)S(1)}, u32[]{:S(2)}, u32[]{:S(2)}) collective-permute-start(bf16[3,16,8,512]{3,2,1,0:T(8,128)(2,1)S(1)} %broadcast_select_fusion.7), channel_id=1, source_target_pairs={{2,0},{3,1},{4,2},{5,3},{6,4},{7,5},{0,6},{1,7},{10,8},{11,9},{12,... | collective-permute-start | bytes 1179656 | tf_op jit(solution)/shard_map/ppermute | solution.py:19
  431.2 42.8 %collective-permute-start.21 = (bf16[3,16,8,512]{3,2,1,0:T(8,128)(2,1)S(1)}, bf16[3,16,8,512]{3,2,1,0:T(8,128)(2,1)S(1)}, u32[]{:S(2)}, u32[]{:S(2)}) collective-permute-start(bf16[3,16,8,512]{3,2,1,0:T(8,128)(2,1)S(1)} %broadcast_select_fusion.8), channel_id=1, source_target_pairs={{4,0},{5,1},{6,2},{7,3},{0,4},{1,5},{2,6},{3,7},{12,8},{13,9},{14,... | collective-permute-start | bytes 1179656 | tf_op jit(solution)/shard_map/ppermute | solution.py:19
  445.1 34.5 %collective-permute-start.9 = (bf16[3,16,8,512]{3,2,1,0:T(8,128)(2,1)S(1)}, bf16[3,16,8,512]{3,2,1,0:T(8,128)(2,1)S(1)}, u32[]{:S(2)}, u32[]{:S(2)}) collective-permute-start(bf16[3,16,8,512]{3,2,1,0:T(8,128)(2,1)S(1)} %broadcast_select_fusion.9), channel_id=1, source_target_pairs={{4,0},{5,1},{6,2},{7,3},{0,4},{1,5},{2,6},{3,7},{12,8},{13,9},{14,... | collective-permute-start | bytes 1179656 | tf_op jit(solution)/shard_map/ppermute | solution.py:19
  474.0 11.3 %collective-permute-start.22 = (bf16[3,16,8,512]{3,2,1,0:T(8,128)(2,1)S(1)}, bf16[3,16,8,512]{3,2,1,0:T(8,128)(2,1)S(1)}, u32[]{:S(2)}, u32[]{:S(2)}) collective-permute-start(bf16[3,16,8,512]{3,2,1,0:T(8,128)(2,1)S(1)} %broadcast_select_fusion.10), channel_id=1, source_target_pairs={{1,0},{2,1},{3,2},{4,3},{5,4},{6,5},{7,6},{0,7},{9,8},{10,9},{11,1... | collective-permute-start | bytes 1179656 | tf_op jit(solution)/shard_map/ppermute | solution.py:19
  479.6 11.0 %collective-permute-start.10 = (bf16[3,16,8,512]{3,2,1,0:T(8,128)(2,1)S(1)}, bf16[3,16,8,512]{3,2,1,0:T(8,128)(2,1)S(1)}, u32[]{:S(2)}, u32[]{:S(2)}) collective-permute-start(bf16[3,16,8,512]{3,2,1,0:T(8,128)(2,1)S(1)} %broadcast_select_fusion.11), channel_id=1, source_target_pairs={{1,0},{2,1},{3,2},{4,3},{5,4},{6,5},{7,6},{0,7},{9,8},{10,9},{11,1... | collective-permute-start | bytes 1179656 | tf_op jit(solution)/shard_map/ppermute | solution.py:19
  (2 other events, 2.0 us)
Sparse Core Ops, SparseCore 0:
  14.1 29.8 all-gather.1
  336.9 44.9 reduce-scatter.1
  491.0 44.1 all-reduce.1
where the time goes:
time: 550 us; the launch traced here: 545 us
  waiting for transfers between devices  152 us (28%)
  local copies, waits for them, and re-layouts  109 us (20%)
  blocking collectives  68.3 us (12%)
  matrix products  68.2 us (12%)
  starting transfers between devices  65.2 us (12%)
  other arithmetic  56.4 us (10%)
  between operations  25.5 us (5%)
    ppermute x24, waiting for transfers between devices, shifted_2(): return lax.ppermute(block, axis, route)  110 us
    ppermute x24, starting transfers between devices, shifted_2(): return lax.ppermute(block, axis, route)  65.1 us
    psum x1, waiting for transfers between devices, on_device(): lax.psum(jnp.concatenate([term_qkv, term_out], axis=1).astype(jnp.bfloat1...  42.4 us
    psum x1, blocking collectives, on_device(): gain_total = lax.psum(jnp.sum(d_hidden * normed, axis=0), ('rad', 'azi'))  37.3 us
    another operation x4, local copies, waits for them, and re-layouts, to_windows(): tensor.reshape(extent_r // WR, WR, extent_a // WA, WA, extent_z // WZ, WZ...  34.3 us
    all_gather x1, blocking collectives, on_device(): lax.all_gather(out_weight, 'azi', axis=0, tiled=True)  31 us
    transpose x2, local copies, waits for them, and re-layouts, from_windows(): windows = windows.transpose(0, 5, 1, 6, 2, 7, 3, 4, 8)  27.4 us
    sub x1, other arithmetic, on_device(): weights = jax.nn.softmax(scores, axis=-1)  19.4 us
  transfers between devices with their start and end apart: 27, of which 15 were waited for; matrix products, arithmetic and copies ran while one was open for 7% of the time, Pallas kernels for 0%

commit v1 on v0

v1 whole, which is shorter than its diff:
```python
import jax
import jax.numpy as jnp
from jax import lax
from jax.experimental import pallas as pl
from jax.experimental.pallas import tpu as pltpu
from jax.sharding import PartitionSpec as P

HEADS = 16
HD = 32
WR = 4
WA = 8
WZ = 8
LANES = 128
LOG2E = 1.4426950408889634

EPS = 1e-05
NT = (((1,), (1,)), ((), ()))
TN = (((0,), (0,)), ((), ()))


def mm(a, b, dims=(((1,), (0,)), ((), ()))):
    return lax.dot_general(a, b, dims, preferred_element_type=jnp.float32)


def block_kernel(
    x_ref, g_ref, gain_ref, wqkv_ref, wout_ref,
    y_ref, dx_ref, gw_ref, gg_ref,
    xhat_s, qkv_s, da_s, att_s, dqkv_s, hid_all, att_all, gs_all, dqkv_all, gain_s,
):
    step = pl.program_id(0)
    steps = pl.num_programs(0)
    width = x_ref.shape[-1]
    tokens = WR * WA * WZ
    x = x_ref[...].astype(jnp.float32).reshape(tokens, width)
    gs_f = g_ref[...].astype(jnp.float32).reshape(tokens, width)
    gs = gs_f.astype(jnp.bfloat16)
    gain = gain_ref[...]
    centred = x - jnp.mean(x, axis=1, keepdims=True)
    inv = lax.rsqrt(jnp.mean(centred * centred, axis=1, keepdims=True) + EPS)
    xhat = centred * inv
    xhat_s[...] = xhat
    hidden = (xhat * gain).astype(jnp.bfloat16)
    qkv_s[...] = mm(hidden, wqkv_ref[...]).astype(jnp.bfloat16)
    da_s[...] = mm(gs, wout_ref[...], NT).astype(jnp.bfloat16)
    scaling = HD ** (-0.5)
    lane = lax.broadcasted_iota(jnp.int32, (1, LANES), 1)
    per_group = LANES // HD

    def group(g, carry):
        base = pl.multiple_of(g * LANES, LANES)
        q = qkv_s[:, pl.ds(base, LANES)]
        k = qkv_s[:, pl.ds(width + base, LANES)]
        v = qkv_s[:, pl.ds(2 * width + base, LANES)]
        da = da_s[:, pl.ds(base, LANES)]
        k_t = k.astype(jnp.float32).T.astype(jnp.bfloat16)
        v_t = v.astype(jnp.float32).T.astype(jnp.bfloat16)
        dv = jnp.zeros((tokens, LANES), jnp.float32)
        dk = jnp.zeros((tokens, LANES), jnp.float32)
        att_t, dq_t = [], []
        for h in range(per_group):
            mine = (lane >= h * HD) & (lane < (h + 1) * HD)
            mask = jnp.where(mine, 1.0, 0.0).astype(jnp.bfloat16)
            qm = q * mask
            dam = da * mask
            s = mm(k, qm, NT) * (scaling * LOG2E)
            e = jnp.exp2(s - jnp.max(s, axis=0, keepdims=True))
            p = e * (1.0 / jnp.sum(e, axis=0, keepdims=True))
            p_low = p.astype(jnp.bfloat16)
            dp = mm(v, dam, NT)
            ds = p * (dp - jnp.sum(p * dp, axis=0, keepdims=True))
            ds = ds.astype(jnp.bfloat16)
            dv += mm(p_low, dam)
            dk += mm(ds, qm)
            att_t.append(mm(v_t[h * HD:(h + 1) * HD], p_low))
            dq_t.append(mm(k_t[h * HD:(h + 1) * HD], ds))
        att_s[:, pl.ds(base, LANES)] = jnp.concatenate(att_t, axis=0).T.astype(jnp.bfloat16)
        dqkv_s[:, pl.ds(base, LANES)] = (
            jnp.concatenate(dq_t, axis=0).T * scaling
        ).astype(jnp.bfloat16)
        dqkv_s[:, pl.ds(width + base, LANES)] = (dk * scaling).astype(jnp.bfloat16)
        dqkv_s[:, pl.ds(2 * width + base, LANES)] = dv.astype(jnp.bfloat16)
        return carry

    lax.fori_loop(0, width // LANES, group, 0)
    att = att_s[...]
    y = x + mm(att, wout_ref[...])
    y_ref[...] = y.reshape(y_ref.shape).astype(jnp.bfloat16)
    d_qkv = dqkv_s[...]
    d_hidden = mm(d_qkv, wqkv_ref[...], NT)
    xhat = xhat_s[...]
    term_gain = jnp.sum(d_hidden * xhat, axis=0, keepdims=True)
    d_normed = d_hidden * gain
    dx = gs_f + inv * (
        d_normed
        - jnp.mean(d_normed, axis=1, keepdims=True)
        - xhat * jnp.mean(d_normed * xhat, axis=1, keepdims=True)
    )
    dx_ref[...] = dx.reshape(dx_ref.shape).astype(jnp.bfloat16)
    here = pl.ds(pl.multiple_of(step * tokens, tokens), tokens)
    hid_all[here, :] = hidden
    att_all[here, :] = att
    gs_all[here, :] = gs
    dqkv_all[here, :] = d_qkv

    @pl.when(step == 0)
    def _():
        gain_s[...] = jnp.zeros_like(gain_s)

    gain_s[...] += term_gain

    @pl.when(step == steps - 1)
    def _():
        gw_ref[:, : 3 * width] = mm(hid_all[...], dqkv_all[...], TN).astype(jnp.bfloat16)
        gw_ref[:, 3 * width:] = mm(att_all[...], gs_all[...], TN).astype(jnp.bfloat16)
        gg_ref[...] = gain_s[...]


def block_pass(x, g, gain, wqkv, wout):
    rows, cols, depth, width = x.shape
    tokens = WR * WA * WZ
    grid_r, grid_a = rows // WR, cols // WA
    number = rows * cols * depth
    field = pl.BlockSpec((WR, WA, depth, width), lambda i: (i // grid_a, i % grid_a, 0, 0))

    def whole(shape):
        return pl.BlockSpec(shape, lambda i: (0,) * len(shape))

    bf, f32 = jnp.bfloat16, jnp.float32
    return pl.pallas_call(
        block_kernel,
        grid=(grid_r * grid_a,),
        in_specs=[field, field, whole((1, width)), whole(wqkv.shape), whole(wout.shape)],
        out_specs=[field, field, whole((width, 4 * width)), whole((1, width))],
        out_shape=[
            jax.ShapeDtypeStruct(x.shape, bf),
            jax.ShapeDtypeStruct(x.shape, bf),
            jax.ShapeDtypeStruct((width, 4 * width), bf),
            jax.ShapeDtypeStruct((1, width), f32),
        ],
        scratch_shapes=[
            pltpu.VMEM((tokens, width), f32),
            pltpu.VMEM((tokens, 3 * width), bf),
            pltpu.VMEM((tokens, width), bf),
            pltpu.VMEM((tokens, width), bf),
            pltpu.VMEM((tokens, 3 * width), bf),
            pltpu.VMEM((number, width), bf),
            pltpu.VMEM((number, width), bf),
            pltpu.VMEM((number, width), bf),
            pltpu.VMEM((number, 3 * width), bf),
            pltpu.VMEM((1, width), f32),
        ],
        compiler_params=pltpu.CompilerParams(vmem_limit_bytes=48 * 1024 * 1024),
        cost_estimate=pl.CostEstimate(
            flops=number * width * width * 24, bytes_accessed=12 * 2 ** 20, transcendentals=0
        ),
        name="block_pass",
    )(x, g, gain, wqkv, wout)


def shifted_2(block, axis, distance):
    devices = range(lax.axis_size(axis))
    route = [((i - distance) % len(devices), i) for i in devices]
    return lax.ppermute(block, axis, route)


def azi_roll(pieces, amount):
    cols_dev = pieces[0].shape[1]
    device_hops = amount // cols_dev
    remainder = amount % cols_dev
    current = pieces
    bit_count = (lax.axis_size("azi") - 1).bit_length()
    for bit_level in range(bit_count):
        hopped = shifted_2((current[0], current[1]), "azi", -(1 << bit_level))
        chosen = device_hops >> bit_level & 1 == 1
        current = (
            jnp.where(chosen, hopped[0], current[0]),
            jnp.where(chosen, hopped[1], current[1]),
        )
    following = shifted_2((current[0], current[1]), "azi", -1)
    return tuple(
        (
            lax.dynamic_slice_in_dim(
                jnp.concatenate([mine, theirs], axis=1), remainder, cols_dev, 1
            )
            for mine, theirs in zip(current, following)
        )
    )


def shift_in(first, second, shift_rad, shift_azi, offset, total_cols):
    rim_rows = WR - 1
    rows_dev, cols_dev, depth, width = first.shape
    below = shifted_2((first[:rim_rows], second[:rim_rows]), "rad", -1)
    extended = (
        jnp.concatenate([first, below[0]], axis=0),
        jnp.concatenate([second, below[1]], axis=0),
    )
    leading = shifted_2((extended[0][:, : WA - 1], extended[1][:, : WA - 1]), "azi", -1)
    rolled = tuple(
        (
            lax.dynamic_slice_in_dim(
                jnp.concatenate([own_part, lead_part], axis=1), shift_azi, cols_dev, 1
            )
            for own_part, lead_part in zip(extended, leading)
        )
    )
    wrapped = azi_roll(below, (offset + shift_azi) % total_cols)
    last_row = lax.axis_index("rad") == lax.axis_size("rad") - 1
    results = []
    for rolled_part, wrapped_part in zip(rolled, wrapped):
        joined = jnp.concatenate(
            [rolled_part[:rows_dev], jnp.where(last_row, wrapped_part, rolled_part[rows_dev:])],
            axis=0,
        )
        results.append(lax.dynamic_slice_in_dim(joined, shift_rad, rows_dev, 0))
    return (results[0], results[1])


def shift_out(first, second, shift_rad, shift_azi, offset, total_cols):
    rim_rows = WR - 1
    rows_dev, cols_dev, depth, width = first.shape
    above = shifted_2((first[rows_dev - rim_rows :], second[rows_dev - rim_rows :]), "rad", 1)
    extended = (
        jnp.concatenate([above[0], first], axis=0),
        jnp.concatenate([above[1], second], axis=0),
    )
    trailing = shifted_2(
        (extended[0][:, cols_dev - (WA - 1) :], extended[1][:, cols_dev - (WA - 1) :]), "azi", 1
    )
    rolled = tuple(
        (
            lax.dynamic_slice_in_dim(
                jnp.concatenate([trail_part, own_part], axis=1), WA - 1 - shift_azi, cols_dev, 1
            )
            for own_part, trail_part in zip(extended, trailing)
        )
    )
    amount = (total_cols - (offset + shift_azi) % total_cols) % total_cols
    wrapped = azi_roll(above, amount)
    first_row = lax.axis_index("rad") == 0
    results = []
    for rolled_part, wrapped_part in zip(rolled, wrapped):
        joined = jnp.concatenate(
            [jnp.where(first_row, wrapped_part, rolled_part[:rim_rows]), rolled_part[rim_rows:]],
            axis=0,
        )
        results.append(lax.dynamic_slice_in_dim(joined, rim_rows - shift_rad, rows_dev, 0))
    return (results[0], results[1])


def on_device(tokens, cotangent, ln_gain, qkv_weight, out_weight, shear_offset, window_shift):
    rows_dev, cols_dev, depth, width = tokens.shape
    assert depth == WZ
    number = rows_dev * cols_dev * depth
    n_rad = lax.axis_size("rad")
    n_azi = lax.axis_size("azi")
    total_cols = cols_dev * n_azi
    shift_rad = window_shift[0]
    shift_azi = window_shift[1]
    offset = shear_offset[0]
    weights = lax.all_gather(
        jnp.concatenate([qkv_weight, out_weight], axis=1), "azi", axis=0, tiled=True
    )
    qkv_full = weights[:, : 3 * width]
    out_full = weights[:, 3 * width :]
    shifted, grad_in = shift_in(tokens, cotangent, shift_rad, shift_azi, offset, total_cols)
    out_shifted, grad_shifted, term, term_gain = block_pass(
        shifted, grad_in, ln_gain.reshape(1, width), qkv_full, out_full
    )
    block_out, grad_tokens = shift_out(
        out_shifted, grad_shifted, shift_rad, shift_azi, offset, total_cols
    )
    share = lax.psum_scatter(term, "azi", scatter_dimension=0, tiled=True)
    share = lax.psum(share, "rad").astype(jnp.float32)
    gain_total = lax.psum(term_gain[0], ("rad", "azi"))
    factor = float(number * n_rad * n_azi) ** (-0.5)
    grad_qkv = share[:, : 3 * width] * factor
    grad_out = share[:, 3 * width :] * factor
    return (block_out, grad_tokens, grad_qkv, grad_out, gain_total * factor)


def solution(mesh):
    in_specs = (
        P("rad", "azi", None, None),
        P("rad", "azi", None, None),
        P(),
        P("azi", None),
        P("azi", None),
        P(),
        P(),
    )
    out_specs = (
        P("rad", "azi", None, None),
        P("rad", "azi", None, None),
        P("azi", None),
        P("azi", None),
        P(),
    )
    return jax.shard_map(
        on_device, mesh=mesh, in_specs=in_specs, out_specs=out_specs, check_vma=False
    )
```

time: 550 us -> 363 us (0.66)
  local copies, waits for them, and re-layouts: 109 us -> 10.1 us
  matrix products: 68.2 us -> 0 us
  Pallas kernels: 0 us -> 43.4 us
  other arithmetic: 56.4 us -> 17.7 us
  waiting for transfers between devices: 152 us -> 182 us
  blocking collectives: 68.3 us -> 40.2 us
  starting transfers between devices: 65.2 us -> 46.8 us
    dot_general x12 -> x0, matrix products: 68.2 us -> none  [the longest x1 14.4 us: on_device(): jnp.einsum('nhqd,nhkd->nhqk', d_windows, values, preferred_element_type=j...]
    another operation x9 -> x0, local copies, waits for them, and re-layouts: 67 us -> none  [the longest x4 34.3 us: to_windows(): tensor.reshape(extent_r // WR, WR, extent_a // WA, WA, extent_z // WZ, WZ...]
    pallas_call x0 -> x1, Pallas kernels: none -> 43.4 us  [block_pass(): pl.pallas_call(block_kernel, grid=(grid_r * grid_a,), in_specs=[field, fi...]
    all_gather x1 -> x0, blocking collectives: 31 us -> none  [on_device(): lax.all_gather(out_weight, 'azi', axis=0, tiled=True)]
    transpose x2 -> x0, local copies, waits for them, and re-layouts: 27.4 us -> none  [from_windows(): windows = windows.transpose(0, 5, 1, 6, 2, 7, 3, 4, 8)]
    ppermute x24, waiting for transfers between devices: 110 us -> 136 us  [shifted_2(): return lax.ppermute(block, axis, route)]
    sub x1 -> x0, other arithmetic: 19.4 us -> none  [on_device(): weights = jax.nn.softmax(scores, axis=-1)]
    ppermute x24, starting transfers between devices: 65.1 us -> 46.6 us  [shifted_2(): return lax.ppermute(block, axis, route)]
  transfers between devices with their start and end apart: 27 -> 27, of which waited for: 15 -> 17; matrix products, arithmetic and copies ran while one was open for 7% -> 5% of each run, Pallas kernels for 0% -> 0%
where the time goes in v1:
time: 363 us; the launch traced here: 362 us
  waiting for transfers between devices  182 us (50%)
  starting transfers between devices  46.8 us (13%)
  Pallas kernels  43.4 us (12%)
  blocking collectives  40.2 us (11%)
  between operations  22 us (6%)
  other arithmetic  17.7 us (5%)
  local copies, waits for them, and re-layouts  10.1 us (3%)
    ppermute x24, waiting for transfers between devices, shifted_2(): return lax.ppermute(block, axis, route)  136 us
    ppermute x24, starting transfers between devices, shifted_2(): return lax.ppermute(block, axis, route)  46.6 us
    psum x1, waiting for transfers between devices, on_device(): share = lax.psum(share, 'rad').astype(jnp.float32)  46.2 us
    pallas_call x1, Pallas kernels, block_pass(): pl.pallas_call(block_kernel, grid=(grid_r * grid_a,), in_specs=[field, fi...  43.4 us
    psum x1, blocking collectives, on_device(): gain_total = lax.psum(term_gain[0], ('rad', 'azi'))  40.2 us
  transfers between devices with their start and end apart: 27, of which 17 were waited for; matrix products, arithmetic and copies ran while one was open for 5% of the time, Pallas kernels for 0%

profile of v1, /device:TPU:0, one launch (start us, length us, event | category | flops | bytes accessed | tf_op | source)
XLA Modules:
  0.0 362.1 jit_solution(2126616986674920097)
XLA Ops:
  7.2 1.8 pad_maximum_fusion
  9.1 1.0 slice.72
  10.1 3.9 %collective-permute-start.6 = (bf16[3,16,8,512]{3,2,1,0:T(8,128)(2,1)S(1)}, bf16[3,16,8,512]{3,2,1,0:T(8,128)(2,1)S(1)}, u32[]{:S(2)}, u32[]{:S(2)}) collective-permute-start(bf16[3,16,8,512]{3,2,1,0:T(8,128)(2,1)S(1)} %slice.72), channel_id=1, source_target_pairs={{8,0},{16,8},{24,16},{0,24},{9,1},{17,9},{25,17},{1,25},{10,2},{18... | collective-permute-start | bytes 1179656 | tf_op jit(solution)/shard_map/ppermute | solution.py:163
  14.0 1.0 slice.67
  15.6 7.9 %collective-permute-done.6 = bf16[3,16,8,512]{3,2,1,0:T(8,128)(2,1)S(1)} collective-permute-done((bf16[3,16,8,512]{3,2,1,0:T(8,128)(2,1)S(1)}, bf16[3,16,8,512]{3,2,1,0:T(8,128)(2,1)S(1)}, u32[]{:S(2)}, u32[]{:S(2)}) %collective-permute-start.6) | collective-permute-done | bytes 393248 | tf_op jit(solution)/shard_map/ppermute | solution.py:163
  23.6 1.1 collective-permute-start.8
  26.6 4.2 %collective-permute-done = bf16[3,16,8,512]{3,2,1,0:T(8,128)(2,1)} collective-permute-done((bf16[3,16,8,512]{3,2,1,0:T(8,128)(2,1)S(1)}, bf16[3,16,8,512]{3,2,1,0:T(8,128)(2,1)}, u32[]{:S(2)}, u32[]{:S(2)}) %collective-permute-start) | collective-permute-done | bytes 393248 | tf_op jit(solution)/shard_map/ppermute | solution.py:163
  30.8 2.3 collective-permute-start.2
  33.1 1.3 constant_dynamic-update-slice_fusion.1
  34.5 3.8 %collective-permute-done.8 = bf16[3,16,8,512]{3,2,1,0:T(8,128)(2,1)} collective-permute-done((bf16[3,16,8,512]{3,2,1,0:T(8,128)(2,1)S(1)}, bf16[3,16,8,512]{3,2,1,0:T(8,128)(2,1)}, u32[]{:S(2)}, u32[]{:S(2)}) %collective-permute-start.8) | collective-permute-done | bytes 393248 | tf_op jit(solution)/shard_map/ppermute | solution.py:163
  38.3 1.2 broadcast_select_fusion
  39.5 2.7 collective-permute-start.9
  42.2 4.5 %collective-permute-done.2 = bf16[3,16,8,512]{3,2,1,0:T(8,128)(2,1)S(1)} collective-permute-done((bf16[3,16,8,512]{3,2,1,0:T(8,128)(2,1)}, bf16[3,16,8,512]{3,2,1,0:T(8,128)(2,1)S(1)}, u32[]{:S(2)}, u32[]{:S(2)}) %collective-permute-start.2) | collective-permute-done | bytes 393248 | tf_op jit(solution)/shard_map/ppermute | solution.py:163
  46.7 1.9 broadcast_select_fusion.1
  48.5 6.1 %collective-permute-start.3 = (bf16[3,16,8,512]{3,2,1,0:T(8,128)(2,1)}, bf16[3,16,8,512]{3,2,1,0:T(8,128)(2,1)}, u32[]{:S(2)}, u32[]{:S(2)}) collective-permute-start(bf16[3,16,8,512]{3,2,1,0:T(8,128)(2,1)} %get-tuple-element.19), channel_id=1, source_target_pairs={{2,0},{3,1},{4,2},{5,3},{6,4},{7,5},{0,6},{1,7},{10,8},{11,9},{12,... | collective-permute-start | bytes 1179656 | tf_op jit(solution)/shard_map/ppermute | solution.py:163
  54.6 0.9 slice.91
  55.5 1.5 collective-permute-start.7
  61.2 4.2 %collective-permute-done.3 = bf16[3,16,8,512]{3,2,1,0:T(8,128)(2,1)} collective-permute-done((bf16[3,16,8,512]{3,2,1,0:T(8,128)(2,1)}, bf16[3,16,8,512]{3,2,1,0:T(8,128)(2,1)}, u32[]{:S(2)}, u32[]{:S(2)}) %collective-permute-start.3) | collective-permute-done | bytes 393248 | tf_op jit(solution)/shard_map/ppermute | solution.py:163
  65.4 1.0 broadcast_select_fusion.3
  66.4 3.5 collective-permute-start.4
  69.9 7.7 %collective-permute-done.7 = bf16[11,7,8,512]{3,2,1,0:T(8,128)(2,1)} collective-permute-done((bf16[11,7,8,512]{3,2,1,0:T(8,128)(2,1)}, bf16[11,7,8,512]{3,2,1,0:T(8,128)(2,1)}, u32[]{:S(2)}, u32[]{:S(2)}) %collective-permute-start.7) | collective-permute-done | bytes 630816 | tf_op jit(solution)/shard_map/ppermute | solution.py:163
  77.7 1.5 fusion.2
  79.1 30.3 %collective-permute-done.10 = bf16[3,16,8,512]{3,2,1,0:T(8,128)(2,1)S(1)} collective-permute-done((bf16[3,16,8,512]{3,2,1,0:T(8,128)(2,1)S(1)}, bf16[3,16,8,512]{3,2,1,0:T(8,128)(2,1)S(1)}, u32[]{:S(2)}, u32[]{:S(2)}) %collective-permute-start.10) | collective-permute-done | bytes 393248 | tf_op jit(solution)/shard_map/ppermute | solution.py:163
  109.6 4.1 %collective-permute-done.4 = bf16[3,16,8,512]{3,2,1,0:T(8,128)(2,1)S(1)} collective-permute-done((bf16[3,16,8,512]{3,2,1,0:T(8,128)(2,1)S(1)}, bf16[3,16,8,512]{3,2,1,0:T(8,128)(2,1)S(1)}, u32[]{:S(2)}, u32[]{:S(2)}) %collective-permute-start.4) | collective-permute-done | bytes 393248 | tf_op jit(solution)/shard_map/ppermute | solution.py:163
  115.5 4.2 %collective-permute-done.5 = bf16[3,16,8,512]{3,2,1,0:T(8,128)(2,1)S(1)} collective-permute-done((bf16[3,16,8,512]{3,2,1,0:T(8,128)(2,1)S(1)}, bf16[3,16,8,512]{3,2,1,0:T(8,128)(2,1)S(1)}, u32[]{:S(2)}, u32[]{:S(2)}) %collective-permute-start.5) | collective-permute-done | bytes 393248 | tf_op jit(solution)/shard_map/ppermute | solution.py:163
  119.9 1.3 fusion.7.x_ref
  121.2 2.8 slice.94.wqkv_ref
  123.9 1.1 slice.95.wout_ref
  125.0 43.4 %block_pass.1 = (bf16[8,16,8,512]{3,2,1,0:T(8,128)(2,1)S(1)}, bf16[8,16,8,512]{3,2,1,0:T(8,128)(2,1)S(1)}, bf16[512,2048]{1,0:T(8,128)(2,1)}, f32[1,512]{1,0:T(1,128)S(1)}) custom-call(bf16[8,16,8,512]{3,2,1,0:T(8,128)(2,1)S(1)} %copy-done, bf16[8,16,8,512]{3,2,1,0:T(8,128)(2,1)S(1)} %fusion.6.g_ref, f32[1,512]{1,0:T(1,128)S(1)} %bitcast.7, ...), custom_call_target="tpu_custom_call" | custom-call | flops 6442450944 | bytes 12582912 | tf_op jit(solution)/shard_map/block_pass/pallas_call | solution.py:129
  168.5 1.8 collective-permute-start.18
  170.3 1.5 collective-permute-start.12
  171.8 8.7 %collective-permute-done.18 = bf16[3,16,8,512]{3,2,1,0:T(8,128)(2,1)} collective-permute-done((bf16[3,16,8,512]{3,2,1,0:T(8,128)(2,1)S(1)}, bf16[3,16,8,512]{3,2,1,0:T(8,128)(2,1)}, u32[]{:S(2)}, u32[]{:S(2)}) %collective-permute-start.18) | collective-permute-done | bytes 393248 | tf_op jit(solution)/shard_map/ppermute | solution.py:163
  180.6 3.8 %collective-permute-start.19 = (bf16[3,16,8,512]{3,2,1,0:T(8,128)(2,1)}, bf16[3,16,8,512]{3,2,1,0:T(8,128)(2,1)S(1)}, u32[]{:S(2)}, u32[]{:S(2)}) collective-permute-start(bf16[3,16,8,512]{3,2,1,0:T(8,128)(2,1)} %collective-permute-done.18), channel_id=1, source_target_pairs={{1,0},{2,1},{3,2},{4,3},{5,4},{6,5},{7,6},{0,7},{9,8},{10,9},{11,1... | collective-permute-start | bytes 1179656 | tf_op jit(solution)/shard_map/ppermute | solution.py:163
  184.3 4.5 %collective-permute-done.12 = bf16[3,16,8,512]{3,2,1,0:T(8,128)(2,1)S(1)} collective-permute-done((bf16[3,16,8,512]{3,2,1,0:T(8,128)(2,1)S(1)}, bf16[3,16,8,512]{3,2,1,0:T(8,128)(2,1)S(1)}, u32[]{:S(2)}, u32[]{:S(2)}) %collective-permute-start.12) | collective-permute-done | bytes 393248 | tf_op jit(solution)/shard_map/ppermute | solution.py:163
  192.2 40.2 %psum.15 = f32[512]{0:T(512)S(1)} all-reduce(f32[512]{0:T(512)S(1)} %bitcast.6), channel_id=1, replica_groups=mesh['rad'=4,'azi'=8] {'rad','azi'}, use_global_device_ids=true, to_apply=%region_2.3 | all-reduce | flops 512 | bytes 4096 | tf_op jit(solution)/shard_map/psum | solution.py:275
  232.4 1.1 constant_dynamic-update-slice_fusion.7
  233.6 2.2 collective-permute-start.20
  236.6 9.1 %collective-permute-done.20 = bf16[3,16,8,512]{3,2,1,0:T(8,128)(2,1)S(1)} collective-permute-done((bf16[3,16,8,512]{3,2,1,0:T(8,128)(2,1)S(1)}, bf16[3,16,8,512]{3,2,1,0:T(8,128)(2,1)S(1)}, u32[]{:S(2)}, u32[]{:S(2)}) %collective-permute-start.20) | collective-permute-done | bytes 393248 | tf_op jit(solution)/shard_map/ppermute | solution.py:163
  246.5 7.3 %collective-permute-done.14 = bf16[3,16,8,512]{3,2,1,0:T(8,128)(2,1)S(1)} collective-permute-done((bf16[3,16,8,512]{3,2,1,0:T(8,128)(2,1)S(1)}, bf16[3,16,8,512]{3,2,1,0:T(8,128)(2,1)S(1)}, u32[]{:S(2)}, u32[]{:S(2)}) %collective-permute-start.14) | collective-permute-done | bytes 393248 | tf_op jit(solution)/shard_map/ppermute | solution.py:163
  253.9 11.9 %collective-permute-start.15 = (bf16[3,16,8,512]{3,2,1,0:T(8,128)(2,1)S(1)}, bf16[3,16,8,512]{3,2,1,0:T(8,128)(2,1)S(1)}, u32[]{:S(2)}, u32[]{:S(2)}) collective-permute-start(bf16[3,16,8,512]{3,2,1,0:T(8,128)(2,1)S(1)} %broadcast_select_fusion.9), channel_id=1, source_target_pairs={{4,0},{5,1},{6,2},{7,3},{0,4},{1,5},{2,6},{3,7},{12,8},{13,9},{14,... | collective-permute-start | bytes 1179656 | tf_op jit(solution)/shard_map/ppermute | solution.py:163
  266.1 1.2 collective-permute-start.17
  267.3 23.6 %collective-permute-done.21 = bf16[3,16,8,512]{3,2,1,0:T(8,128)(2,1)S(1)} collective-permute-done((bf16[3,16,8,512]{3,2,1,0:T(8,128)(2,1)S(1)}, bf16[3,16,8,512]{3,2,1,0:T(8,128)(2,1)S(1)}, u32[]{:S(2)}, u32[]{:S(2)}) %collective-permute-start.21) | collective-permute-done | bytes 393248 | tf_op jit(solution)/shard_map/ppermute | solution.py:163
  291.0 7.7 %collective-permute-done.15 = bf16[3,16,8,512]{3,2,1,0:T(8,128)(2,1)S(1)} collective-permute-done((bf16[3,16,8,512]{3,2,1,0:T(8,128)(2,1)S(1)}, bf16[3,16,8,512]{3,2,1,0:T(8,128)(2,1)S(1)}, u32[]{:S(2)}, u32[]{:S(2)}) %collective-permute-start.15) | collective-permute-done | bytes 393248 | tf_op jit(solution)/shard_map/ppermute | solution.py:163
  300.5 3.7 %collective-permute-done.16 = bf16[3,16,8,512]{3,2,1,0:T(8,128)(2,1)S(1)} collective-permute-done((bf16[3,16,8,512]{3,2,1,0:T(8,128)(2,1)S(1)}, bf16[3,16,8,512]{3,2,1,0:T(8,128)(2,1)S(1)}, u32[]{:S(2)}, u32[]{:S(2)}) %collective-permute-start.16) | collective-permute-done | bytes 393248 | tf_op jit(solution)/shard_map/ppermute | solution.py:163
  304.5 1.2 fusion.4
  305.7 1.2 fusion.5
  306.9 46.2 %all-reduce.2.cloned.1.call-done = bf16[64,2048]{1,0:T(8,128)(2,1)} async-done(((bf16[64,2048]{1,0:T(8,128)(2,1)}), bf16[64,2048]{1,0:T(8,128)(2,1)}) %all-reduce.2.cloned.1.call-update) | async-done | bytes 262160 | tf_op jit(solution)/shard_map/psum | solution.py:274
  353.1 1.0 convert_element_type.3
  (75 shorter events, 10.1 us)
Async XLA Ops:
  7.2 19.4 %copy-start.4 = (bf16[8,16,8,512]{3,2,1,0:T(8,128)(2,1)S(1)}, bf16[8,16,8,512]{3,2,1,0:T(8,128)(2,1)}, u32[]{:S(2)}) copy-start(bf16[8,16,8,512]{3,2,1,0:T(8,128)(2,1)} %param.8) | copy-start | bytes 3145732
  7.2 18.1 %copy-start.6 = (s32[3]{0:T(128)S(1)}, s32[3]{0:T(128)}, u32[]{:S(2)}) copy-start(s32[3]{0:T(128)} %param.13) | copy-start | bytes 40
  7.2 114.0 %all-gather.2.cloned.1.call-start = ((), (), s32[]{:S(2)}) async-start(), calls=%async_computation.1 | async-start | bytes 2359296 | tf_op jit(solution)/shard_map/all_gather | solution.py:261
  9.0 295.4 %reduce-scatter.2.cloned.1.call-start = ((), (), s32[]{:S(2)}) async-start(), calls=%async_computation.2 | async-start | bytes 2359296 | tf_op jit(solution)/shard_map/reduce_scatter | solution.py:273
  10.1 13.5 %collective-permute-start.6 = (bf16[3,16,8,512]{3,2,1,0:T(8,128)(2,1)S(1)}, bf16[3,16,8,512]{3,2,1,0:T(8,128)(2,1)S(1)}, u32[]{:S(2)}, u32[]{:S(2)}) collective-permute-start(bf16[3,16,8,512]{3,2,1,0:T(8,128)(2,1)S(1)} %slice.72), channel_id=1, source_target_pairs={{8,0},{16,8},{24,16},{0,24},{9,1},{17,9},{25,17},{1,25},{10,2},{18... | collective-permute-start | bytes 1179656 | tf_op jit(solution)/shard_map/ppermute | solution.py:163
  15.1 15.8 %collective-permute-start = (bf16[3,16,8,512]{3,2,1,0:T(8,128)(2,1)S(1)}, bf16[3,16,8,512]{3,2,1,0:T(8,128)(2,1)}, u32[]{:S(2)}, u32[]{:S(2)}) collective-permute-start(bf16[3,16,8,512]{3,2,1,0:T(8,128)(2,1)S(1)} %slice.67), channel_id=1, source_target_pairs={{8,0},{16,8},{24,16},{0,24},{9,1},{17,9},{25,17},{1,25},{10,2},{18... | collective-permute-start | bytes 1179656 | tf_op jit(solution)/shard_map/ppermute | solution.py:163
  23.6 10.9 %copy-start.5 = (bf16[3,16,8,512]{3,2,1,0:T(8,128)(2,1)}, bf16[3,16,8,512]{3,2,1,0:T(8,128)(2,1)S(1)}, u32[]{:S(2)}) copy-start(bf16[3,16,8,512]{3,2,1,0:T(8,128)(2,1)S(1)} %collective-permute-done.6) | copy-start | bytes 1179652
  23.6 14.7 %collective-permute-start.8 = (bf16[3,16,8,512]{3,2,1,0:T(8,128)(2,1)S(1)}, bf16[3,16,8,512]{3,2,1,0:T(8,128)(2,1)}, u32[]{:S(2)}, u32[]{:S(2)}) collective-permute-start(bf16[3,16,8,512]{3,2,1,0:T(8,128)(2,1)S(1)} %collective-permute-done.6), channel_id=1, source_target_pairs={{1,0},{2,1},{3,2},{4,3},{5,4},{6,5},{7,6},{0,7},{9,8},{10,9},{11,1... | collective-permute-start | bytes 1179656 | tf_op jit(solution)/shard_map/ppermute | solution.py:163
  30.8 15.8 %collective-permute-start.2 = (bf16[3,16,8,512]{3,2,1,0:T(8,128)(2,1)}, bf16[3,16,8,512]{3,2,1,0:T(8,128)(2,1)S(1)}, u32[]{:S(2)}, u32[]{:S(2)}) collective-permute-start(bf16[3,16,8,512]{3,2,1,0:T(8,128)(2,1)} %collective-permute-done), channel_id=1, source_target_pairs={{1,0},{2,1},{3,2},{4,3},{5,4},{6,5},{7,6},{0,7},{9,8},{10,9},{11,1... | collective-permute-start | bytes 1179656 | tf_op jit(solution)/shard_map/ppermute | solution.py:163
  39.5 21.5 %collective-permute-start.9 = (bf16[3,16,8,512]{3,2,1,0:T(8,128)(2,1)S(1)}, bf16[3,16,8,512]{3,2,1,0:T(8,128)(2,1)}, u32[]{:S(2)}, u32[]{:S(2)}) collective-permute-start(bf16[3,16,8,512]{3,2,1,0:T(8,128)(2,1)S(1)} %get-tuple-element.17), channel_id=1, source_target_pairs={{2,0},{3,1},{4,2},{5,3},{6,4},{7,5},{0,6},{1,7},{10,8},{11,9},{12,... | collective-permute-start | bytes 1179656 | tf_op jit(solution)/shard_map/ppermute | solution.py:163
  48.5 16.9 %collective-permute-start.3 = (bf16[3,16,8,512]{3,2,1,0:T(8,128)(2,1)}, bf16[3,16,8,512]{3,2,1,0:T(8,128)(2,1)}, u32[]{:S(2)}, u32[]{:S(2)}) collective-permute-start(bf16[3,16,8,512]{3,2,1,0:T(8,128)(2,1)} %get-tuple-element.19), channel_id=1, source_target_pairs={{2,0},{3,1},{4,2},{5,3},{6,4},{7,5},{0,6},{1,7},{10,8},{11,9},{12,... | collective-permute-start | bytes 1179656 | tf_op jit(solution)/shard_map/ppermute | solution.py:163
  55.5 22.1 %collective-permute-start.7 = (bf16[11,7,8,512]{3,2,1,0:T(8,128)(2,1)}, bf16[11,7,8,512]{3,2,1,0:T(8,128)(2,1)}, u32[]{:S(2)}, u32[]{:S(2)}) collective-permute-start(bf16[11,7,8,512]{3,2,1,0:T(8,128)(2,1)} %slice.91), channel_id=1, source_target_pairs={{1,0},{2,1},{3,2},{4,3},{5,4},{6,5},{7,6},{0,7},{9,8},{10,9},{11,1... | collective-permute-start | bytes 1892360 | tf_op jit(solution)/shard_map/ppermute | solution.py:163
  61.0 53.4 %collective-permute-start.1 = (bf16[11,7,8,512]{3,2,1,0:T(8,128)(2,1)S(1)}, bf16[11,7,8,512]{3,2,1,0:T(8,128)(2,1)S(1)}, u32[]{:S(2)}, u32[]{:S(2)}) collective-permute-start(bf16[11,7,8,512]{3,2,1,0:T(8,128)(2,1)S(1)} %slice.88), channel_id=1, source_target_pairs={{1,0},{2,1},{3,2},{4,3},{5,4},{6,5},{7,6},{0,7},{9,8},{10,9},{11,1... | collective-permute-start | bytes 1892360 | tf_op jit(solution)/shard_map/ppermute | solution.py:163
  61.1 48.3 %collective-permute-start.10 = (bf16[3,16,8,512]{3,2,1,0:T(8,128)(2,1)S(1)}, bf16[3,16,8,512]{3,2,1,0:T(8,128)(2,1)S(1)}, u32[]{:S(2)}, u32[]{:S(2)}) collective-permute-start(bf16[3,16,8,512]{3,2,1,0:T(8,128)(2,1)S(1)} %broadcast_select_fusion.2), channel_id=1, source_target_pairs={{4,0},{5,1},{6,2},{7,3},{0,4},{1,5},{2,6},{3,7},{12,8},{13,9},{14,... | collective-permute-start | bytes 1179656 | tf_op jit(solution)/shard_map/ppermute | solution.py:163
  66.4 47.2 %collective-permute-start.4 = (bf16[3,16,8,512]{3,2,1,0:T(8,128)(2,1)S(1)}, bf16[3,16,8,512]{3,2,1,0:T(8,128)(2,1)S(1)}, u32[]{:S(2)}, u32[]{:S(2)}) collective-permute-start(bf16[3,16,8,512]{3,2,1,0:T(8,128)(2,1)S(1)} %broadcast_select_fusion.3), channel_id=1, source_target_pairs={{4,0},{5,1},{6,2},{7,3},{0,4},{1,5},{2,6},{3,7},{12,8},{13,9},{14,... | collective-permute-start | bytes 1179656 | tf_op jit(solution)/shard_map/ppermute | solution.py:163
  109.5 5.5 %collective-permute-start.11 = (bf16[3,16,8,512]{3,2,1,0:T(8,128)(2,1)S(1)}, bf16[3,16,8,512]{3,2,1,0:T(8,128)(2,1)S(1)}, u32[]{:S(2)}, u32[]{:S(2)}) collective-permute-start(bf16[3,16,8,512]{3,2,1,0:T(8,128)(2,1)S(1)} %broadcast_select_fusion.4), channel_id=1, source_target_pairs={{1,0},{2,1},{3,2},{4,3},{5,4},{6,5},{7,6},{0,7},{9,8},{10,9},{11,1... | collective-permute-start | bytes 1179656 | tf_op jit(solution)/shard_map/ppermute | solution.py:163
  113.7 6.0 %collective-permute-start.5 = (bf16[3,16,8,512]{3,2,1,0:T(8,128)(2,1)S(1)}, bf16[3,16,8,512]{3,2,1,0:T(8,128)(2,1)S(1)}, u32[]{:S(2)}, u32[]{:S(2)}) collective-permute-start(bf16[3,16,8,512]{3,2,1,0:T(8,128)(2,1)S(1)} %broadcast_select_fusion.5), channel_id=1, source_target_pairs={{1,0},{2,1},{3,2},{4,3},{5,4},{6,5},{7,6},{0,7},{9,8},{10,9},{11,1... | collective-permute-start | bytes 1179656 | tf_op jit(solution)/shard_map/ppermute | solution.py:163
  121.2 3.8 %copy-start.1 = (f32[512]{0:T(512)S(1)}, f32[512]{0:T(512)}, u32[]{:S(2)}) copy-start(f32[512]{0:T(512)} %param.9) | copy-start | bytes 6148
  121.2 3.8 %copy-start = (bf16[8,16,8,512]{3,2,1,0:T(8,128)(2,1)S(1)}, bf16[8,16,8,512]{3,2,1,0:T(8,128)(2,1)}, u32[]{:S(2)}) copy-start(bf16[8,16,8,512]{3,2,1,0:T(8,128)(2,1)} %fusion.7.x_ref) | copy-start | bytes 3145732
  168.4 184.7 %all-reduce.2.cloned.1.call-start = ((), (), s32[]{:S(2)}) async-start(), calls=%async_computation.3 | async-start | bytes 524288 | tf_op jit(solution)/shard_map/psum | solution.py:274
  168.5 12.1 %collective-permute-start.18 = (bf16[3,16,8,512]{3,2,1,0:T(8,128)(2,1)S(1)}, bf16[3,16,8,512]{3,2,1,0:T(8,128)(2,1)}, u32[]{:S(2)}, u32[]{:S(2)}) collective-permute-start(bf16[3,16,8,512]{3,2,1,0:T(8,128)(2,1)S(1)} %slice.82), channel_id=1, source_target_pairs={{24,0},{0,8},{8,16},{16,24},{25,1},{1,9},{9,17},{17,25},{26,2},{2,... | collective-permute-start | bytes 1179656 | tf_op jit(solution)/shard_map/ppermute | solution.py:163
  170.3 18.6 %collective-permute-start.12 = (bf16[3,16,8,512]{3,2,1,0:T(8,128)(2,1)S(1)}, bf16[3,16,8,512]{3,2,1,0:T(8,128)(2,1)S(1)}, u32[]{:S(2)}, u32[]{:S(2)}) collective-permute-start(bf16[3,16,8,512]{3,2,1,0:T(8,128)(2,1)S(1)} %slice.78), channel_id=1, source_target_pairs={{24,0},{0,8},{8,16},{16,24},{25,1},{1,9},{9,17},{17,25},{26,2},{2,... | collective-permute-start | bytes 1179656 | tf_op jit(solution)/shard_map/ppermute | solution.py:163
  180.6 51.9 %collective-permute-start.19 = (bf16[3,16,8,512]{3,2,1,0:T(8,128)(2,1)}, bf16[3,16,8,512]{3,2,1,0:T(8,128)(2,1)S(1)}, u32[]{:S(2)}, u32[]{:S(2)}) collective-permute-start(bf16[3,16,8,512]{3,2,1,0:T(8,128)(2,1)} %collective-permute-done.18), channel_id=1, source_target_pairs={{1,0},{2,1},{3,2},{4,3},{5,4},{6,5},{7,6},{0,7},{9,8},{10,9},{11,1... | collective-permute-start | bytes 1179656 | tf_op jit(solution)/shard_map/ppermute | solution.py:163
  188.9 46.9 %collective-permute-start.13 = (bf16[3,16,8,512]{3,2,1,0:T(8,128)(2,1)S(1)}, bf16[3,16,8,512]{3,2,1,0:T(8,128)(2,1)S(1)}, u32[]{:S(2)}, u32[]{:S(2)}) collective-permute-start(bf16[3,16,8,512]{3,2,1,0:T(8,128)(2,1)S(1)} %collective-permute-done.12), channel_id=1, source_target_pairs={{1,0},{2,1},{3,2},{4,3},{5,4},{6,5},{7,6},{0,7},{9,8},{10,9},{11,1... | collective-permute-start | bytes 1179656 | tf_op jit(solution)/shard_map/ppermute | solution.py:163
  233.6 12.1 %collective-permute-start.20 = (bf16[3,16,8,512]{3,2,1,0:T(8,128)(2,1)S(1)}, bf16[3,16,8,512]{3,2,1,0:T(8,128)(2,1)S(1)}, u32[]{:S(2)}, u32[]{:S(2)}) collective-permute-start(bf16[3,16,8,512]{3,2,1,0:T(8,128)(2,1)S(1)} %get-tuple-element.14), channel_id=1, source_target_pairs={{2,0},{3,1},{4,2},{5,3},{6,4},{7,5},{0,6},{1,7},{10,8},{11,9},{12,... | collective-permute-start | bytes 1179656 | tf_op jit(solution)/shard_map/ppermute | solution.py:163
  235.9 17.9 %collective-permute-start.14 = (bf16[3,16,8,512]{3,2,1,0:T(8,128)(2,1)S(1)}, bf16[3,16,8,512]{3,2,1,0:T(8,128)(2,1)S(1)}, u32[]{:S(2)}, u32[]{:S(2)}) collective-permute-start(bf16[3,16,8,512]{3,2,1,0:T(8,128)(2,1)S(1)} %get-tuple-element.16), channel_id=1, source_target_pairs={{2,0},{3,1},{4,2},{5,3},{6,4},{7,5},{0,6},{1,7},{10,8},{11,9},{12,... | collective-permute-start | bytes 1179656 | tf_op jit(solution)/shard_map/ppermute | solution.py:163
  245.7 45.2 %collective-permute-start.21 = (bf16[3,16,8,512]{3,2,1,0:T(8,128)(2,1)S(1)}, bf16[3,16,8,512]{3,2,1,0:T(8,128)(2,1)S(1)}, u32[]{:S(2)}, u32[]{:S(2)}) collective-permute-start(bf16[3,16,8,512]{3,2,1,0:T(8,128)(2,1)S(1)} %broadcast_select_fusion.8), channel_id=1, source_target_pairs={{4,0},{5,1},{6,2},{7,3},{0,4},{1,5},{2,6},{3,7},{12,8},{13,9},{14,... | collective-permute-start | bytes 1179656 | tf_op jit(solution)/shard_map/ppermute | solution.py:163
  253.9 44.9 %collective-permute-start.15 = (bf16[3,16,8,512]{3,2,1,0:T(8,128)(2,1)S(1)}, bf16[3,16,8,512]{3,2,1,0:T(8,128)(2,1)S(1)}, u32[]{:S(2)}, u32[]{:S(2)}) collective-permute-start(bf16[3,16,8,512]{3,2,1,0:T(8,128)(2,1)S(1)} %broadcast_select_fusion.9), channel_id=1, source_target_pairs={{4,0},{5,1},{6,2},{7,3},{0,4},{1,5},{2,6},{3,7},{12,8},{13,9},{14,... | collective-permute-start | bytes 1179656 | tf_op jit(solution)/shard_map/ppermute | solution.py:163
  265.9 33.0 %collective-permute-start.23 = (bf16[11,7,8,512]{3,2,1,0:T(8,128)(2,1)S(1)}, bf16[11,7,8,512]{3,2,1,0:T(8,128)(2,1)S(1)}, u32[]{:S(2)}, u32[]{:S(2)}) collective-permute-start(bf16[11,7,8,512]{3,2,1,0:T(8,128)(2,1)S(1)} %slice.99), channel_id=1, source_target_pairs={{7,0},{0,1},{1,2},{2,3},{3,4},{4,5},{5,6},{6,7},{15,8},{8,9},{9,10... | collective-permute-start | bytes 1892360 | tf_op jit(solution)/shard_map/ppermute | solution.py:163
  266.1 33.1 %collective-permute-start.17 = (bf16[11,7,8,512]{3,2,1,0:T(8,128)(2,1)S(1)}, bf16[11,7,8,512]{3,2,1,0:T(8,128)(2,1)S(1)}, u32[]{:S(2)}, u32[]{:S(2)}) collective-permute-start(bf16[11,7,8,512]{3,2,1,0:T(8,128)(2,1)S(1)} %slice.96), channel_id=1, source_target_pairs={{7,0},{0,1},{1,2},{2,3},{3,4},{4,5},{5,6},{6,7},{15,8},{8,9},{9,10... | collective-permute-start | bytes 1892360 | tf_op jit(solution)/shard_map/ppermute | solution.py:163
  291.0 8.6 %collective-permute-start.22 = (bf16[3,16,8,512]{3,2,1,0:T(8,128)(2,1)S(1)}, bf16[3,16,8,512]{3,2,1,0:T(8,128)(2,1)S(1)}, u32[]{:S(2)}, u32[]{:S(2)}) collective-permute-start(bf16[3,16,8,512]{3,2,1,0:T(8,128)(2,1)S(1)} %broadcast_select_fusion.10), channel_id=1, source_target_pairs={{1,0},{2,1},{3,2},{4,3},{5,4},{6,5},{7,6},{0,7},{9,8},{10,9},{11,1... | collective-permute-start | bytes 1179656 | tf_op jit(solution)/shard_map/ppermute | solution.py:163
  298.8 5.4 %collective-permute-start.16 = (bf16[3,16,8,512]{3,2,1,0:T(8,128)(2,1)S(1)}, bf16[3,16,8,512]{3,2,1,0:T(8,128)(2,1)S(1)}, u32[]{:S(2)}, u32[]{:S(2)}) collective-permute-start(bf16[3,16,8,512]{3,2,1,0:T(8,128)(2,1)S(1)} %broadcast_select_fusion.11), channel_id=1, source_target_pairs={{1,0},{2,1},{3,2},{4,3},{5,4},{6,5},{7,6},{0,7},{9,8},{10,9},{11,1... | collective-permute-start | bytes 1179656 | tf_op jit(solution)/shard_map/ppermute | solution.py:163
  299.2 1.1 copy-start.3
  299.5 4.7 %copy-start.2 = (bf16[11,16,8,512]{3,2,1,0:T(8,128)(2,1)}, bf16[11,16,8,512]{3,2,1,0:T(8,128)(2,1)S(1)}, u32[]{:S(2)}) copy-start(bf16[11,16,8,512]{3,2,1,0:T(8,128)(2,1)S(1)} %fusion.1) | copy-start | bytes 4325380
  300.5 4.0 %slice-start.1 = ((bf16[11,16,8,512]{3,2,1,0:T(8,128)(2,1)}), bf16[8,16,8,512]{3,2,1,0:T(8,128)(2,1)S(1)}, s32[]{:S(2)}) async-start(bf16[11,16,8,512]{3,2,1,0:T(8,128)(2,1)} %copy-done.3), calls=%async_computation.5 | async-start | bytes 2097152 | tf_op jit(solution)/shard_map/slice | solution.py:244
  304.4 1.3 slice-start
Sparse Core Ops, SparseCore 0:
  10.2 35.0 all-gather.1
  168.5 40.5 reduce-scatter.1
  304.6 48.4 all-reduce.1
